TPU v7x, 32 devices: a whole 2x2x4 slice. The times are simulated.
32 devices in a mesh: dp: 8 (over z, x), tensor: 4 (over y, core).
Axes of the slice: x: 2, y: 2, z: 4, core: 2. Of those that a mesh axis runs over, the one named last changes fastest.
Arguments:
- query_input: bfloat16 [12288, 768], P(('dp', 'tensor')), may hold values from -6 to 6
- key_input: bfloat16 [12288, 768], P(('dp', 'tensor')), may hold values from -6 to 6
- query_length: int32 [48], P('dp'), may hold values from 128 to 256, as said below
- key_length: int32 [48], P('dp'), may hold values from 128 to 256, as said below
- pair_count: int32 [8], P('dp'), may hold values from 1 to 6, as said below
- query_qkv: bfloat16 [2, 768, 3, 768], P(None, None, None, 'tensor'), may hold values from -0.21875 to 0.21875
- query_qv_bias: float32 [2, 2, 768], P(None, None, 'tensor'), may hold values from -1.8 to 1.8
- query_out: bfloat16 [2, 768, 768], P(None, 'tensor'), may hold values from -1.5 to 1.5
- query_in: bfloat16 [2, 768, 3072], P(None, None, 'tensor'), may hold values from -0.21875 to 0.21875
- query_in_bias: float32 [2, 3072], P(None, 'tensor'), may hold values from -1.8 to 1.8
- query_down: bfloat16 [2, 3072, 768], P(None, 'tensor'), may hold values from -0.109375 to 0.109375
- query_gain: float32 [2, 2, 768], replicated, may hold values from 0.5 to 1.5
- query_shift: float32 [2, 4, 768], replicated, may hold values from -0.6 to 0.6
- key_qkv: bfloat16 [2, 768, 3, 768], P(None, None, None, 'tensor'), may hold values from -0.21875 to 0.21875
- key_qv_bias: float32 [2, 2, 768], P(None, None, 'tensor'), may hold values from -1.8 to 1.8
- key_out: bfloat16 [2, 768, 768], P(None, 'tensor'), may hold values from -1.5 to 1.5
- key_in: bfloat16 [2, 768, 3072], P(None, None, 'tensor'), may hold values from -0.21875 to 0.21875
- key_in_bias: float32 [2, 3072], P(None, 'tensor'), may hold values from -1.8 to 1.8
- key_down: bfloat16 [2, 3072, 768], P(None, 'tensor'), may hold values from -0.109375 to 0.109375
- key_gain: float32 [2, 2, 768], replicated, may hold values from 0.5 to 1.5
- key_shift: float32 [2, 4, 768], replicated, may hold values from -0.6 to 0.6
Outputs:
- per_pair: float32 [48], P('dp')
- query_grad: float32 [12288, 768], P(('dp', 'tensor'))
- grad_qkv: float32 [2, 768, 3, 768], P(None, 'dp', None, 'tensor')
- grad_out: float32 [2, 768, 768], P(None, 'tensor', 'dp')
- grad_in: float32 [2, 768, 3072], P(None, 'dp', 'tensor')
- grad_down: float32 [2, 3072, 768], P(None, 'tensor', 'dp')
- grad_qv_bias: float32 [2, 2, 768], replicated
- grad_in_bias: float32 [2, 3072], replicated
- grad_gain: float32 [2, 2, 768], replicated
- grad_shift: float32 [2, 4, 768], replicated
Inputs may be any that keep to these rules, and one draw needn't show every extreme that they name: `query_length`: unpadded tokens of each query crop; some crop of every draw has all 256. `key_length`: unpadded tokens of each key crop; some crop of every draw has all 256. `pair_count`: live pairs of an index of dp; some index has all 6 live.
All inputs are finite; a program needn't handle non-finite values.
Results may differ from a plain program's by a relative error of at most 0.019.
Values may be sent and summed in bfloat16 or wider, within the bound.
A program may use at most 192 MiB of HBM per device.

v0:
```python
from functools import partial

import jax
import jax.numpy as jnp
from jax import lax
from jax.sharding import PartitionSpec as P

D = 768
HEADS = 12
FF = 3072
SEQ = 256
LAYERS = 2


norm_eps = 1e-06
temper = 0.05
masked_fill = -1e30


def matmul_plain(left, right):
    return jnp.dot(left, right, preferred_element_type=jnp.float32)


def matmul_right(left, right):
    return lax.dot_general(
        left, right, (((1,), (1,)), ((), ())), preferred_element_type=jnp.float32
    )


def matmul_left(left, right):
    return lax.dot_general(
        left, right, (((0,), (0,)), ((), ())), preferred_element_type=jnp.float32
    )


def exact_left(left, right):
    return lax.dot_general(
        left,
        right,
        (((0,), (0,)), ((), ())),
        precision=lax.Precision.HIGHEST,
        preferred_element_type=jnp.float32,
    )


def exact_plain(left, right):
    return jnp.dot(left, right, precision=lax.Precision.HIGHEST, preferred_element_type=jnp.float32)


def exact_right(left, right):
    return lax.dot_general(
        left,
        right,
        (((1,), (1,)), ((), ())),
        precision=lax.Precision.HIGHEST,
        preferred_element_type=jnp.float32,
    )


def layer_norm(values, gain, shift):
    center = values - jnp.mean(values, axis=-1, keepdims=True)
    spread = jnp.mean(center * center, axis=-1, keepdims=True)
    return center * lax.rsqrt(spread + norm_eps) * gain + shift


def normalize(values):
    return values * lax.rsqrt(jnp.sum(values * values, axis=1, keepdims=True) + norm_eps)


def split_heads(projected, crops, head_dim):
    local_width = projected.shape[1] // 3
    heads_here = local_width // head_dim
    parts = projected.reshape(crops, SEQ, 3, heads_here, head_dim)
    return (parts[:, :, 0], parts[:, :, 1], parts[:, :, 2])


def score_block(queries, keys_part, lengths, scale):
    scores = (
        jnp.einsum("cqhe,ckhe->chqk", queries, keys_part, preferred_element_type=jnp.float32)
        * scale
    )
    position = lax.broadcasted_iota(jnp.int32, (1, 1, 1, SEQ), 3)
    visible = position < lengths[:, None, None, None]
    return (jnp.where(visible, scores, masked_fill), visible)


def forward_layer(x_share, weights, layer, lengths, head_dim):
    qkv_w, qv_bias, out_w, in_w, in_bias, down_w, gains, shifts = weights
    local_width = qkv_w.shape[3]
    crops = lengths.shape[0]
    flat_w = qkv_w[layer].reshape(qkv_w.shape[1], 3 * local_width)
    bias_row = jnp.stack(
        [qv_bias[layer, 0], jnp.zeros((local_width,), jnp.float32), qv_bias[layer, 1]]
    ).reshape(3 * local_width)
    piece = lax.all_gather(x_share.astype(jnp.bfloat16), "tensor", axis=0, tiled=True)
    projected = (matmul_plain(piece, flat_w) + bias_row).astype(jnp.bfloat16)
    hidden = piece
    queries, keys_part, values = split_heads(projected, crops, head_dim)
    scores, visible = score_block(queries, keys_part, lengths, head_dim ** (-0.5))
    highest = jnp.max(scores, axis=3, keepdims=True)
    exponent = jnp.exp(scores - highest)
    total = jnp.sum(exponent, axis=3, keepdims=True)
    log_total = highest + jnp.log(total)
    probs_low = (exponent / total).astype(jnp.bfloat16)
    mixed = jnp.einsum("chqk,ckhe->cqhe", probs_low, values, preferred_element_type=jnp.float32)
    mixed = mixed.reshape(crops * SEQ, local_width).astype(jnp.bfloat16)
    out_layer = out_w[layer]
    attended = lax.psum_scatter(
        matmul_plain(mixed, out_layer), "tensor", scatter_dimension=0, tiled=True
    )
    resid = x_share + attended + shifts[layer, 0]
    normed = layer_norm(resid, gains[layer, 0], shifts[layer, 1])
    in_layer = in_w[layer]
    in_row = in_bias[layer]
    piece = lax.all_gather(normed.astype(jnp.bfloat16), "tensor", axis=0, tiled=True)
    inner = matmul_plain(piece, in_layer) + in_row
    active, inner, normed_full = (
        jax.nn.gelu(inner, approximate=False).astype(jnp.bfloat16),
        inner,
        piece,
    )
    down_layer = down_w[layer]
    reduced = lax.psum_scatter(
        matmul_plain(active, down_layer), "tensor", scatter_dimension=0, tiled=True
    )
    combined = normed + reduced + shifts[layer, 2]
    output = layer_norm(combined, gains[layer, 1], shifts[layer, 3])
    kept = (hidden, projected, log_total, mixed, resid, normed_full, inner, active, combined)
    return (output, kept)


def backward_layer(grad_output, weights, layer, lengths, head_dim, kept):
    qkv_w, qv_bias, out_w, in_w, in_bias, down_w, gains, shifts = weights
    hidden, projected, log_total, mixed, resid, normed_full, inner, active, combined = kept
    crops = lengths.shape[0]
    rows_all = hidden.shape[0]
    local_width = qkv_w.shape[3]
    scale = head_dim ** (-0.5)
    unused, norm_two_back = jax.vjp(layer_norm, combined, gains[layer, 1], shifts[layer, 3])
    grad_combined, grad_gain_two, grad_shift_three = norm_two_back(grad_output)
    down_layer = down_w[layer]
    piece = lax.all_gather(grad_combined.astype(jnp.bfloat16), "tensor", axis=0, tiled=True)
    grad_active = matmul_right(piece, down_layer)
    grad_branch_full = piece
    grad_down = matmul_left(active, grad_branch_full)
    unused_inner, gelu_back = jax.vjp(partial(jax.nn.gelu, approximate=False), inner)
    grad_inner = gelu_back(grad_active)[0].astype(jnp.bfloat16)
    grad_in_bias = jnp.sum(grad_inner.astype(jnp.float32), axis=0)
    grad_in = matmul_left(normed_full, grad_inner)
    in_layer = in_w[layer]
    grad_normed = grad_combined + lax.psum_scatter(
        matmul_right(grad_inner, in_layer), "tensor", scatter_dimension=0, tiled=True
    )
    unused_norm, norm_one_back = jax.vjp(layer_norm, resid, gains[layer, 0], shifts[layer, 1])
    grad_resid, grad_gain_one, grad_shift_one = norm_one_back(grad_normed)
    out_layer = out_w[layer]
    piece = lax.all_gather(grad_resid.astype(jnp.bfloat16), "tensor", axis=0, tiled=True)
    grad_mixed = matmul_right(piece, out_layer)
    grad_out_w = matmul_left(mixed, piece)
    queries, keys_part, values = split_heads(projected, crops, head_dim)
    heads_here = local_width // head_dim
    grad_mixed_low = grad_mixed.astype(jnp.bfloat16).reshape(crops, SEQ, heads_here, head_dim)
    scores, visible = score_block(queries, keys_part, lengths, scale)
    probs = jnp.where(visible, jnp.exp(scores - log_total), 0.0)
    probs_low = probs.astype(jnp.bfloat16)
    grad_probs = jnp.einsum(
        "cqhe,ckhe->chqk", grad_mixed_low, values, preferred_element_type=jnp.float32
    )
    inner_sum = jnp.sum(probs * grad_probs, axis=3, keepdims=True)
    grad_scores = (probs * (grad_probs - inner_sum)).astype(jnp.bfloat16)
    grad_queries = (
        jnp.einsum("chqk,ckhe->cqhe", grad_scores, keys_part, preferred_element_type=jnp.float32)
        * scale
    )
    grad_keys = (
        jnp.einsum("chqk,cqhe->ckhe", grad_scores, queries, preferred_element_type=jnp.float32)
        * scale
    )
    grad_values = jnp.einsum(
        "chqk,cqhe->ckhe", probs_low, grad_mixed_low, preferred_element_type=jnp.float32
    )
    grad_projected = (
        jnp.stack([grad_queries, grad_keys, grad_values], axis=2)
        .reshape(rows_all, 3 * local_width)
        .astype(jnp.bfloat16)
    )
    bias_sums = jnp.sum(
        grad_projected.astype(jnp.float32).reshape(rows_all, 3, local_width), axis=0
    )
    grad_qv = jnp.stack([bias_sums[0], bias_sums[2]])
    grad_qkv = matmul_left(hidden, grad_projected).reshape(hidden.shape[1], 3, local_width)
    flat_w = qkv_w[layer].reshape(qkv_w.shape[1], 3 * local_width)
    grad_x = grad_resid + lax.psum_scatter(
        matmul_right(grad_projected, flat_w), "tensor", scatter_dimension=0, tiled=True
    )
    grad_gains = jnp.stack([grad_gain_one, grad_gain_two])
    grad_shifts = jnp.stack(
        [
            jnp.sum(grad_resid, axis=0),
            grad_shift_one,
            jnp.sum(grad_combined, axis=0),
            grad_shift_three,
        ]
    )
    matrices = (grad_qkv, grad_out_w, grad_in, grad_down)
    vectors = (grad_qv, grad_in_bias, grad_gains, grad_shifts)
    return (grad_x, matrices, vectors)


def on_device(
    query_input,
    key_input,
    query_length,
    key_length,
    pair_count,
    query_qkv,
    query_qv_bias,
    query_out,
    query_in,
    query_in_bias,
    query_down,
    query_gain,
    query_shift,
    key_qkv,
    key_qv_bias,
    key_out,
    key_in,
    key_in_bias,
    key_down,
    key_gain,
    key_shift,
):
    head_dim = D // HEADS
    query_weights = (
        query_qkv,
        query_qv_bias,
        query_out,
        query_in,
        query_in_bias,
        query_down,
        query_gain,
        query_shift,
    )
    key_weights = (
        key_qkv,
        key_qv_bias,
        key_out,
        key_in,
        key_in_bias,
        key_down,
        key_gain,
        key_shift,
    )
    x_query = query_input.astype(jnp.float32)
    x_key = key_input.astype(jnp.float32)
    kept_all = []
    for layer in range(LAYERS):
        x_query, kept = forward_layer(x_query, query_weights, layer, query_length, head_dim)
        kept_all.append(kept)
        x_key, unused = forward_layer(x_key, key_weights, layer, key_length, head_dim)
    share = x_query.shape[0]
    slots = query_length.shape[0]
    tensor_pos = lax.axis_index("tensor")
    global_row = tensor_pos * share + lax.broadcasted_iota(jnp.int32, (share, 1), 0)
    crop_of = global_row // SEQ
    place = global_row % SEQ
    member = crop_of == lax.broadcasted_iota(jnp.int32, (1, slots), 1)

    def pool_mask(lengths):
        reach = jnp.sum(jnp.where(member, lengths[None, :], 0), axis=1, keepdims=True)
        return jnp.where(member & (place < reach), 1.0, 0.0).astype(jnp.float32)

    query_mask = pool_mask(query_length)
    key_mask = pool_mask(key_length)
    sum_query, sum_key = lax.psum(
        (exact_left(query_mask, x_query), exact_left(key_mask, x_key)), "tensor"
    )
    mean_query = sum_query / query_length[:, None].astype(jnp.float32)
    unit_query, normalize_back = jax.vjp(normalize, mean_query)
    unit_key = normalize(sum_key / key_length[:, None].astype(jnp.float32))
    all_keys, counts = (
        lax.all_gather(unit_key, "dp", axis=0, tiled=True),
        lax.all_gather(pair_count.astype(jnp.float32), "dp", axis=0, tiled=True),
    )
    pairs = all_keys.shape[0]
    groups = counts.shape[0]
    column = lax.broadcasted_iota(jnp.int32, (1, pairs), 1)
    owner = column // slots == lax.broadcasted_iota(jnp.int32, (groups, 1), 0)
    limit = jnp.sum(jnp.where(owner, counts[:, None], 0.0), axis=0, keepdims=True)
    live_slot = (column % slots).astype(jnp.float32) < limit
    logits = exact_right(unit_query, all_keys) / temper
    masked = jnp.where(live_slot, logits, masked_fill)
    highest = jnp.max(masked, axis=1, keepdims=True)
    exponent = jnp.exp(masked - highest)
    total = jnp.sum(exponent, axis=1, keepdims=True)
    log_total = highest[:, 0] + jnp.log(total[:, 0])
    probs = exponent / total
    slot_ids = lax.broadcasted_iota(jnp.int32, (slots, 1), 0)
    own_mask = column == lax.axis_index("dp") * slots + slot_ids
    own_logit = jnp.sum(jnp.where(own_mask, logits, 0.0), axis=1)
    mine_live = slot_ids[:, 0] < pair_count[0]
    per_pair = jnp.where(mine_live, log_total - own_logit, 0.0)
    weighting = jnp.where(mine_live[:, None], probs - own_mask.astype(jnp.float32), 0.0) * (
        SEQ / temper
    )
    grad_unit = exact_plain(weighting, all_keys)
    grad_mean = normalize_back(grad_unit)[0]
    grad_sum = grad_mean / query_length[:, None].astype(jnp.float32)
    grad_x = exact_plain(query_mask, grad_sum)
    collected = [None] * LAYERS
    for layer in reversed(range(LAYERS)):
        grad_x, matrices, vectors = backward_layer(
            grad_x, query_weights, layer, query_length, head_dim, kept_all[layer]
        )
        collected[layer] = (matrices, vectors)
    stacked = tuple((jnp.stack([entry[0][index] for entry in collected]) for index in range(4)))
    weight_parts = (
        lax.psum_scatter(stacked[0], "dp", scatter_dimension=1, tiled=True),
        lax.psum_scatter(stacked[1], "dp", scatter_dimension=2, tiled=True),
        lax.psum_scatter(stacked[2], "dp", scatter_dimension=1, tiled=True),
        lax.psum_scatter(stacked[3], "dp", scatter_dimension=2, tiled=True),
    )
    local_width = query_qv_bias.shape[2]
    inner_width = query_in_bias.shape[1]
    qv_stack = jnp.stack([entry[1][0] for entry in collected])
    in_stack = jnp.stack([entry[1][1] for entry in collected])
    gain_stack = jnp.stack([entry[1][2] for entry in collected])
    shift_stack = jnp.stack([entry[1][3] for entry in collected])
    qv_full = lax.dynamic_update_slice(
        jnp.zeros((LAYERS, 2, D), jnp.float32), qv_stack, (0, 0, tensor_pos * local_width)
    )
    in_full = lax.dynamic_update_slice(
        jnp.zeros((LAYERS, FF), jnp.float32), in_stack, (0, tensor_pos * inner_width)
    )
    grad_qv_bias, grad_in_bias, grad_gain, grad_shift = lax.psum(
        (qv_full, in_full, gain_stack, shift_stack), ("dp", "tensor")
    )
    return (
        per_pair,
        grad_x,
        weight_parts[0],
        weight_parts[1],
        weight_parts[2],
        weight_parts[3],
        grad_qv_bias,
        grad_in_bias,
        grad_gain,
        grad_shift,
    )


def solution(mesh):
    return jax.shard_map(
        on_device,
        mesh=mesh,
        in_specs=(
            P(("dp", "tensor"), None),
            P(("dp", "tensor"), None),
            P("dp"),
            P("dp"),
            P("dp"),
            P(None, None, None, "tensor"),
            P(None, None, "tensor"),
            P(None, "tensor", None),
            P(None, None, "tensor"),
            P(None, "tensor"),
            P(None, "tensor", None),
            P(),
            P(),
            P(None, None, None, "tensor"),
            P(None, None, "tensor"),
            P(None, "tensor", None),
            P(None, None, "tensor"),
            P(None, "tensor"),
            P(None, "tensor", None),
            P(),
            P(),
        ),
        out_specs=(
            P("dp"),
            P(("dp", "tensor"), None),
            P(None, "dp", None, "tensor"),
            P(None, "tensor", "dp"),
            P(None, "dp", "tensor"),
            P(None, "tensor", "dp"),
            P(),
            P(),
            P(),
            P(),
        ),
        check_vma=False,
    )
```

profile of v0, /device:TPU:29, one launch (start us, length us, event | category | flops | bytes accessed | tf_op | source)
XLA Modules:
  0.0 1697.1 jit_solution(10623219959271457648)
XLA Ops:
  12.6 21.5 %all-gather.14.cloned.1.call-done = bf16[1536,768]{1,0:T(8,128)(2,1)} async-done(((bf16[384,768]{1,0:T(8,128)(2,1)}), bf16[1536,768]{1,0:T(8,128)(2,1)}) %all-gather.14.cloned.1.call-update) | async-done | bytes 2359312 | tf_op jit(solution)/shard_map/all_gather | solution.py:95
  53.9 45.7 %reduce-scatter.20.cloned.1.call-done = f32[384,768]{1,0:T(8,128)} async-done(((f32[1536,768]{1,0:T(8,128)}), f32[384,768]{1,0:T(8,128)}) %reduce-scatter.20.cloned.1.call-update) | async-done | bytes 1179664 | tf_op jit(solution)/shard_map/reduce_scatter | solution.py:108
  103.1 24.0 %all-gather.16.cloned.1.call-done = bf16[1536,768]{1,0:T(8,128)(2,1)} async-done(((bf16[384,768]{1,0:T(8,128)(2,1)}), bf16[1536,768]{1,0:T(8,128)(2,1)}) %all-gather.16.cloned.1.call-update) | async-done | bytes 2359312 | tf_op jit(solution)/shard_map/all_gather | solution.py:115
  127.1 15.0 multiply_convert_fusion.3
  147.9 47.6 %reduce-scatter.22.cloned.1.call-done = f32[384,768]{1,0:T(8,128)} async-done(((f32[1536,768]{1,0:T(8,128)}), f32[384,768]{1,0:T(8,128)}) %reduce-scatter.22.cloned.1.call-update) | async-done | bytes 1179664 | tf_op jit(solution)/shard_map/reduce_scatter | solution.py:123
  198.9 24.3 %all-gather.18.cloned.1.call-done = bf16[1536,768]{1,0:T(8,128)(2,1)} async-done(((bf16[384,768]{1,0:T(8,128)(2,1)}), bf16[1536,768]{1,0:T(8,128)(2,1)}) %all-gather.18.cloned.1.call-update) | async-done | bytes 2359312 | tf_op jit(solution)/shard_map/all_gather | solution.py:95
  244.4 46.8 %reduce-scatter.24.cloned.1.call-done = f32[384,768]{1,0:T(8,128)} async-done(((f32[1536,768]{1,0:T(8,128)}), f32[384,768]{1,0:T(8,128)}) %reduce-scatter.24.cloned.1.call-update) | async-done | bytes 1179664 | tf_op jit(solution)/shard_map/reduce_scatter | solution.py:108
  296.5 20.9 %all-gather.22.cloned.1.call-done = bf16[1536,768]{1,0:T(8,128)(2,1)} async-done(((bf16[384,768]{1,0:T(8,128)(2,1)}), bf16[1536,768]{1,0:T(8,128)(2,1)}) %all-gather.22.cloned.1.call-update) | async-done | bytes 2359312 | tf_op jit(solution)/shard_map/all_gather | solution.py:95
  343.7 15.0 multiply_convert_fusion.2
  366.3 27.5 %reduce-scatter.28.cloned.1.call-done = f32[384,768]{1,0:T(8,128)} async-done(((f32[1536,768]{1,0:T(8,128)}), f32[384,768]{1,0:T(8,128)}) %reduce-scatter.28.cloned.1.call-update) | async-done | bytes 1179664 | tf_op jit(solution)/shard_map/reduce_scatter | solution.py:108
  393.9 50.3 %reduce-scatter.26.cloned.1.call-done = f32[384,768]{1,0:T(8,128)} async-done(((f32[1536,768]{1,0:T(8,128)}), f32[384,768]{1,0:T(8,128)}) %reduce-scatter.26.cloned.1.call-update) | async-done | bytes 1179664 | tf_op jit(solution)/shard_map/reduce_scatter | solution.py:123
  450.6 23.6 %all-gather.24.cloned.1.call-done = bf16[1536,768]{1,0:T(8,128)(2,1)} async-done(((bf16[384,768]{1,0:T(8,128)(2,1)}), bf16[1536,768]{1,0:T(8,128)(2,1)}) %all-gather.24.cloned.1.call-update) | async-done | bytes 2359312 | tf_op jit(solution)/shard_map/all_gather | solution.py:115
  474.1 17.9 %fusion.57 = f32[1536,768]{1,0:T(8,128)} fusion(bf16[1536,768]{1,0:T(8,128)(2,1)} %all-gather.24.cloned.1.call-done, f32[768]{0:T(1024)S(1)} %get-tuple-element.89, bf16[2,768,768]{2,1,0:T(8,128)(2,1)} %param.39, bf16[2,768,768]{2,1,0:T(8,128)(2,1)} %param.37), kind=kOutput, calls=%fused_computation.138 | convolution fusion | flops 3701735424 | bytes 9440256 | tf_op jit(solution)/shard_map/dot_general | solution.py:21
  492.1 47.6 %reduce-scatter.30.cloned.1.call-done = f32[384,768]{1,0:T(8,128)} async-done(((f32[1536,768]{1,0:T(8,128)}), f32[384,768]{1,0:T(8,128)}) %reduce-scatter.30.cloned.1.call-update) | async-done | bytes 1179664 | tf_op jit(solution)/shard_map/reduce_scatter | solution.py:123
  543.2 24.5 %all-gather.26.cloned.1.call-done = bf16[1536,768]{1,0:T(8,128)(2,1)} async-done(((bf16[384,768]{1,0:T(8,128)(2,1)}), bf16[1536,768]{1,0:T(8,128)(2,1)}) %all-gather.26.cloned.1.call-update) | async-done | bytes 2359312 | tf_op jit(solution)/shard_map/all_gather | solution.py:95
  586.0 47.5 %reduce-scatter.32.cloned.1.call-done = f32[384,768]{1,0:T(8,128)} async-done(((f32[1536,768]{1,0:T(8,128)}), f32[384,768]{1,0:T(8,128)}) %reduce-scatter.32.cloned.1.call-update) | async-done | bytes 1179664 | tf_op jit(solution)/shard_map/reduce_scatter | solution.py:108
  636.9 24.4 %all-gather.28.cloned.1.call-done = bf16[1536,768]{1,0:T(8,128)(2,1)} async-done(((bf16[384,768]{1,0:T(8,128)(2,1)}), bf16[1536,768]{1,0:T(8,128)(2,1)}) %all-gather.28.cloned.1.call-update) | async-done | bytes 2359312 | tf_op jit(solution)/shard_map/all_gather | solution.py:115
  661.3 18.1 %fusion.56 = f32[1536,768]{1,0:T(8,128)} fusion(bf16[1536,768]{1,0:T(8,128)(2,1)} %all-gather.28.cloned.1.call-done, f32[768]{0:T(1024)S(1)} %copy-done.137, bf16[2,768,768]{2,1,0:T(8,128)(2,1)} %param.39, bf16[2,768,768]{2,1,0:T(8,128)(2,1)} %param.37), kind=kOutput, calls=%fused_computation.137 | convolution fusion | flops 3701735424 | bytes 9440256 | tf_op jit(solution)/shard_map/dot_general | solution.py:21
  708.2 18.9 %reduce-scatter.34.cloned.1.call-done = f32[384,768]{1,0:T(8,128)} async-done(((f32[1536,768]{1,0:T(8,128)}), f32[384,768]{1,0:T(8,128)}) %reduce-scatter.34.cloned.1.call-update) | async-done | bytes 1179664 | tf_op jit(solution)/shard_map/reduce_scatter | solution.py:123
  741.2 21.6 %all-gather = f32[8,6,768]{2,1,0:T(8,128)S(1)} all-gather(f32[1,6,768]{2,1,0:T(8,128)S(1)} %multiply_bitcast_fusion), channel_id=1, replica_groups=mesh['dp'=8,'tensor'=4] {'dp'}, dimensions={0}, use_global_device_ids=true | all-gather | bytes 165888 | tf_op jit(solution)/shard_map/all_gather | solution.py:282
  769.6 34.7 %all-gather.30.cloned.1.call-done = bf16[1536,768]{1,0:T(8,128)(2,1)} async-done(((bf16[384,768]{1,0:T(8,128)(2,1)}), bf16[1536,768]{1,0:T(8,128)(2,1)}) %all-gather.30.cloned.1.call-update) | async-done | bytes 2359312 | tf_op jit(solution)/shard_map/all_gather | solution.py:142
  819.0 47.6 %reduce-scatter.36.cloned.1.call-done = f32[384,768]{1,0:T(8,128)} async-done(((f32[1536,768]{1,0:T(8,128)}), f32[384,768]{1,0:T(8,128)}) %reduce-scatter.36.cloned.1.call-update) | async-done | bytes 1179664 | tf_op jit(solution)/shard_map/reduce_scatter | solution.py:151
  871.5 24.4 %all-gather.32.cloned.1.call-done = bf16[1536,768]{1,0:T(8,128)(2,1)} async-done(((bf16[384,768]{1,0:T(8,128)(2,1)}), bf16[1536,768]{1,0:T(8,128)(2,1)}) %all-gather.32.cloned.1.call-update) | async-done | bytes 2359312 | tf_op jit(solution)/shard_map/all_gather | solution.py:157
  916.3 47.5 %reduce-scatter.38.cloned.1.call-done = f32[384,768]{1,0:T(8,128)} async-done(((f32[1536,768]{1,0:T(8,128)}), f32[384,768]{1,0:T(8,128)}) %reduce-scatter.38.cloned.1.call-update) | async-done | bytes 1179664 | tf_op jit(solution)/shard_map/reduce_scatter | solution.py:193
  968.7 24.4 %all-gather.34.cloned.1.call-done = bf16[1536,768]{1,0:T(8,128)(2,1)} async-done(((bf16[384,768]{1,0:T(8,128)(2,1)}), bf16[1536,768]{1,0:T(8,128)(2,1)}) %all-gather.34.cloned.1.call-update) | async-done | bytes 2359312 | tf_op jit(solution)/shard_map/all_gather | solution.py:142
  1007.8 47.6 %reduce-scatter.40.cloned.1.call-done = f32[384,768]{1,0:T(8,128)} async-done(((f32[1536,768]{1,0:T(8,128)}), f32[384,768]{1,0:T(8,128)}) %reduce-scatter.40.cloned.1.call-update) | async-done | bytes 1179664 | tf_op jit(solution)/shard_map/reduce_scatter | solution.py:151
  1145.4 112.4 %all-reduce.7.cloned.1.call-done = f32[2,768,768]{1,0,2:T(2,128)} async-done(((f32[2,768,768]{1,0,2:T(2,128)}), f32[2,768,768]{1,0,2:T(2,128)}) %all-reduce.7.cloned.1.call-update) | async-done | bytes 4718608
  1262.5 61.0 %reduce-scatter.48.cloned.1.call-done = f32[96,384]{1,0:T(8,128)} async-done(((f32[768,384]{1,0:T(8,128)}), f32[96,384]{1,0:T(8,128)}) %reduce-scatter.48.cloned.1.call-update) | async-done | bytes 147472
  1325.4 81.6 %reduce-scatter.46.cloned.1.call-done = f32[96,1152]{1,0:T(8,128)} async-done(((f32[768,1152]{1,0:T(8,128)}), f32[96,1152]{1,0:T(8,128)}) %reduce-scatter.46.cloned.1.call-update) | async-done | bytes 442384
  1409.6 48.1 %reduce-scatter.42.cloned.1.call-done = f32[384,768]{1,0:T(8,128)} async-done(((f32[1536,768]{1,0:T(8,128)}), f32[384,768]{1,0:T(8,128)}) %reduce-scatter.42.cloned.1.call-update) | async-done | bytes 1179664 | tf_op jit(solution)/shard_map/reduce_scatter | solution.py:193
  1460.1 97.0 %reduce-scatter.44.cloned.1.call-done = f32[2,96,768]{2,1,0:T(8,128)} async-done(((f32[2,768,768]{2,1,0:T(8,128)}), f32[2,96,768]{2,1,0:T(8,128)}) %reduce-scatter.44.cloned.1.call-update) | async-done | bytes 589840 | tf_op jit(solution)/shard_map/reduce_scatter | solution.py:320
  1557.1 127.9 %all-reduce.9.cloned.1.call-done = (f32[2,2,768]{2,1,0:T(2,128)}, f32[2,3072]{1,0:T(2,128)}, f32[2,2,768]{2,1,0:T(2,128)}, f32[2,4,768]{2,1,0:T(4,128)}) async-done(((f32[2,2,768]{2,1,0:T(2,128)}, f32[2,3072]{1,0:T(2,128)}, f32[2,2,768]{2,1,0:T(2,128)}, f32[2,4,768]{2,1,0:T(4,128)}), (f32[2,2,768]{2,1,0:T(2,128)}, f32[2,3072]{1,0:T(2,128)}, f32[2,2,768]{2,1,0:T(2,128)}, ...) | async-done | bytes 73744 | tf_op jit(solution)/shard_map/psum | solution.py:335
  (624 shorter events, 342.5 us)
Async XLA Ops:
  7.2 26.9 %all-gather.14.cloned.1.call-start = ((), (), s32[]{:S(2)}) async-start(), calls=%async_computation.15 | async-start | bytes 2949120 | tf_op jit(solution)/shard_map/all_gather | solution.py:95
  7.9 91.6 %reduce-scatter.20.cloned.1.call-start = ((), (), s32[]{:S(2)}) async-start(), calls=%async_computation.16 | async-start | bytes 5898240 | tf_op jit(solution)/shard_map/reduce_scatter | solution.py:108
  51.9 75.2 %all-gather.16.cloned.1.call-start = ((), (), s32[]{:S(2)}) async-start(), calls=%async_computation.17 | async-start | bytes 2949120 | tf_op jit(solution)/shard_map/all_gather | solution.py:115
  53.2 238.0 %copy-start.60 = (f32[768]{0:T(1024)}, f32[768]{0:T(1024)S(1)}, u32[]{:S(2)}) copy-start(f32[768]{0:T(1024)S(1)} %get-tuple-element.79) | copy-start | bytes 9220
  53.9 239.4 %copy-start.84 = (f32[768]{0:T(1024)}, f32[768]{0:T(1024)S(1)}, u32[]{:S(2)}) copy-start(f32[768]{0:T(1024)S(1)} %get-tuple-element.63) | copy-start | bytes 9220
  102.5 92.9 %reduce-scatter.22.cloned.1.call-start = ((), (), s32[]{:S(2)}) async-start(), calls=%async_computation.18 | async-start | bytes 5898240 | tf_op jit(solution)/shard_map/reduce_scatter | solution.py:123
  103.1 240.6 %copy-start.135 = (f32[768]{0:T(1024)}, f32[768]{0:T(1024)S(1)}, u32[]{:S(2)}) copy-start(f32[768]{0:T(1024)S(1)} %get-tuple-element.86) | copy-start | bytes 9220
  147.8 75.4 %all-gather.18.cloned.1.call-start = ((), (), s32[]{:S(2)}) async-start(), calls=%async_computation.19 | async-start | bytes 2949120 | tf_op jit(solution)/shard_map/all_gather | solution.py:95
  198.6 92.6 %reduce-scatter.24.cloned.1.call-start = ((), (), s32[]{:S(2)}) async-start(), calls=%async_computation.20 | async-start | bytes 5898240 | tf_op jit(solution)/shard_map/reduce_scatter | solution.py:108
  243.6 73.8 %all-gather.22.cloned.1.call-start = ((), (), s32[]{:S(2)}) async-start(), calls=%async_computation.23 | async-start | bytes 2949120 | tf_op jit(solution)/shard_map/all_gather | solution.py:95
  244.4 99.3 %all-gather.20.cloned.1.call-start = ((), (), s32[]{:S(2)}) async-start(), calls=%async_computation.21 | async-start | bytes 2949120 | tf_op jit(solution)/shard_map/all_gather | solution.py:115
  294.4 99.5 %reduce-scatter.28.cloned.1.call-start = ((), (), s32[]{:S(2)}) async-start(), calls=%async_computation.24 | async-start | bytes 5898240 | tf_op jit(solution)/shard_map/reduce_scatter | solution.py:108
  333.2 110.9 %reduce-scatter.26.cloned.1.call-start = ((), (), s32[]{:S(2)}) async-start(), calls=%async_computation.22 | async-start | bytes 5898240 | tf_op jit(solution)/shard_map/reduce_scatter | solution.py:123
  364.4 109.8 %all-gather.24.cloned.1.call-start = ((), (), s32[]{:S(2)}) async-start(), calls=%async_computation.25 | async-start | bytes 2949120 | tf_op jit(solution)/shard_map/all_gather | solution.py:115
  449.5 90.2 %reduce-scatter.30.cloned.1.call-start = ((), (), s32[]{:S(2)}) async-start(), calls=%async_computation.26 | async-start | bytes 5898240 | tf_op jit(solution)/shard_map/reduce_scatter | solution.py:123
  492.0 75.6 %all-gather.26.cloned.1.call-start = ((), (), s32[]{:S(2)}) async-start(), calls=%async_computation.27 | async-start | bytes 2949120 | tf_op jit(solution)/shard_map/all_gather | solution.py:95
  543.0 90.5 %reduce-scatter.32.cloned.1.call-start = ((), (), s32[]{:S(2)}) async-start(), calls=%async_computation.28 | async-start | bytes 5898240 | tf_op jit(solution)/shard_map/reduce_scatter | solution.py:108
  585.9 75.4 %all-gather.28.cloned.1.call-start = ((), (), s32[]{:S(2)}) async-start(), calls=%async_computation.29 | async-start | bytes 2949120 | tf_op jit(solution)/shard_map/all_gather | solution.py:115
  636.7 90.4 %reduce-scatter.34.cloned.1.call-start = ((), (), s32[]{:S(2)}) async-start(), calls=%async_computation.30 | async-start | bytes 5898240 | tf_op jit(solution)/shard_map/reduce_scatter | solution.py:123
  679.5 124.8 %all-gather.30.cloned.1.call-start = ((), (), s32[]{:S(2)}) async-start(), calls=%async_computation.31 | async-start | bytes 2949120 | tf_op jit(solution)/shard_map/all_gather | solution.py:142
  769.5 97.0 %reduce-scatter.36.cloned.1.call-start = ((), (), s32[]{:S(2)}) async-start(), calls=%async_computation.32 | async-start | bytes 5898240 | tf_op jit(solution)/shard_map/reduce_scatter | solution.py:151
  818.9 76.9 %all-gather.32.cloned.1.call-start = ((), (), s32[]{:S(2)}) async-start(), calls=%async_computation.33 | async-start | bytes 2949120 | tf_op jit(solution)/shard_map/all_gather | solution.py:157
  871.2 92.7 %reduce-scatter.38.cloned.1.call-start = ((), (), s32[]{:S(2)}) async-start(), calls=%async_computation.34 | async-start | bytes 5898240 | tf_op jit(solution)/shard_map/reduce_scatter | solution.py:193
  916.3 76.8 %all-gather.34.cloned.1.call-start = ((), (), s32[]{:S(2)}) async-start(), calls=%async_computation.35 | async-start | bytes 2949120 | tf_op jit(solution)/shard_map/all_gather | solution.py:142
  968.5 86.9 %reduce-scatter.40.cloned.1.call-start = ((), (), s32[]{:S(2)}) async-start(), calls=%async_computation.36 | async-start | bytes 5898240 | tf_op jit(solution)/shard_map/reduce_scatter | solution.py:151
  1007.8 77.9 %all-gather.36.cloned.1.call-start = ((), (), s32[]{:S(2)}) async-start(), calls=%async_computation.37 | async-start | bytes 2949120 | tf_op jit(solution)/shard_map/all_gather | solution.py:157
  1061.0 196.9 %all-reduce.7.cloned.1.call-start = ((), (), s32[]{:S(2)}) async-start(), calls=%async_computation.42 | async-start | bytes 9437184
  1078.7 244.8 %reduce-scatter.48.cloned.1.call-start = ((), (), s32[]{:S(2)}) async-start(), calls=%async_computation.41 | async-start | bytes 1327104
  1101.1 305.9 %reduce-scatter.46.cloned.1.call-start = ((), (), s32[]{:S(2)}) async-start(), calls=%async_computation.40 | async-start | bytes 3981312
  1128.3 329.3 %reduce-scatter.42.cloned.1.call-start = ((), (), s32[]{:S(2)}) async-start(), calls=%async_computation.38 | async-start | bytes 5898240 | tf_op jit(solution)/shard_map/reduce_scatter | solution.py:193
  1134.2 422.9 %reduce-scatter.44.cloned.1.call-start = ((), (), s32[]{:S(2)}) async-start(), calls=%async_computation.39 | async-start | bytes 5308416 | tf_op jit(solution)/shard_map/reduce_scatter | solution.py:320
  1143.8 541.2 %all-reduce.9.cloned.1.call-start = ((), (), s32[]{:S(2)}) async-start(), calls=%async_computation.43 | async-start | bytes 147456 | tf_op jit(solution)/shard_map/psum | solution.py:335
  (163 other events, 4061.6 us)
Sparse Core Ops, SparseCore 0:
  9.6 24.4 all-gather.13
  52.1 47.4 reduce-scatter.19
  102.6 24.4 all-gather.15
  147.9 47.4 reduce-scatter.21
  198.7 24.4 all-gather.17
  243.7 47.4 reduce-scatter.23
  292.8 24.4 all-gather.21
  319.6 24.0 all-gather.19
  346.4 47.4 reduce-scatter.27
  396.2 47.8 reduce-scatter.25
  449.6 24.4 all-gather.23
  492.2 47.4 reduce-scatter.29
  543.1 24.4 all-gather.25
  586.1 47.4 reduce-scatter.31
  636.8 24.4 all-gather.27
  679.6 47.4 reduce-scatter.33
  769.6 34.5 all-gather.29
  819.0 47.4 reduce-scatter.35
  871.3 24.4 all-gather.31
  916.4 47.4 reduce-scatter.37
  968.6 24.4 all-gather.33
  1007.9 47.4 reduce-scatter.39
  1061.1 24.4 all-gather.35
  1089.5 168.3 all-reduce.6
  1261.6 61.7 reduce-scatter.47
  1327.4 79.5 reduce-scatter.45
  1409.5 48.0 reduce-scatter.41
  1461.9 95.2 reduce-scatter.43
  1564.5 120.4 all-reduce.8
where the time goes:
time: 1710 us; the launch traced here: 1700 us
  waiting for transfers between devices  1260 us (74%)
  matrix products  198 us (12%)
  local copies, waits for them, and re-layouts  94.2 us (6%)
  other arithmetic  75.6 us (4%)
  blocking collectives  46.1 us (3%)
  between operations  18 us (1%)
    unnamed x32, waiting for transfers between devices  257 us
    reduce_scatter x4, waiting for transfers between devices, forward_layer(): lax.psum_scatter(matmul_plain(mixed, out_layer), 'tensor', scatter_dimens...  168 us
    reduce_scatter x4, waiting for transfers between devices, forward_layer(): lax.psum_scatter(matmul_plain(active, down_layer), 'tensor', scatter_dime...  164 us
    psum x1, waiting for transfers between devices, on_device(): lax.psum((qv_full, in_full, gain_stack, shift_stack), ('dp', 'tensor'))  128 us
    dot_general x14, matrix products, matmul_plain(): return jnp.dot(left, right, preferred_element_type=jnp.float32)  104 us
    reduce_scatter x1, waiting for transfers between devices, on_device(): lax.psum_scatter(stacked[2], 'dp', scatter_dimension=1, tiled=True)  97 us
    reduce_scatter x2, waiting for transfers between devices, backward_layer(): lax.psum_scatter(matmul_right(grad_projected, flat_w), 'tensor', scatter_...  95.6 us
    reduce_scatter x2, waiting for transfers between devices, backward_layer(): lax.psum_scatter(matmul_right(grad_inner, in_layer), 'tensor', scatter_di...  95.1 us
  transfers between devices with their start and end apart: 29, of which 29 were waited for; matrix products, arithmetic and copies ran while one was open for 9% of the time, Pallas kernels for 0%

commit v1 on v0

v1 whole, which is shorter than its diff:
```python
import functools
import math

import jax
import jax.numpy as jnp
from jax import lax
from jax.experimental import pallas as pl
from jax.experimental.pallas import tpu as pltpu
from jax.sharding import PartitionSpec as P

D = 768
HEAD = 64
SEQ = 256
LAYERS = 2
BLOB = 768
EPS = 1e-06
TEMPER = 0.05
FILL = -1e30
BF = jnp.bfloat16
F32 = jnp.float32
MESH = pl.DeviceIdType.MESH
SCALE = HEAD ** (-0.5)
MIB = 2**20


def mm(a, b):
    return jnp.dot(a, b, preferred_element_type=F32)


def mm_nt(a, b):
    return lax.dot_general(a, b, (((1,), (1,)), ((), ())), preferred_element_type=F32)


def mm_tn(a, b):
    return lax.dot_general(a, b, (((0,), (0,)), ((), ())), preferred_element_type=F32)


def norm(v, gain, shift):
    center = v - jnp.mean(v, axis=-1, keepdims=True)
    rate = lax.rsqrt(jnp.mean(center * center, axis=-1, keepdims=True) + EPS)
    xhat = center * rate
    return xhat, rate, xhat * gain + shift


def norm_back(g, xhat, rate, gain):
    gx = g * gain
    return rate * (
        gx
        - jnp.mean(gx, axis=-1, keepdims=True)
        - xhat * jnp.mean(gx * xhat, axis=-1, keepdims=True)
    )


def rows(v):
    return jnp.sum(v, axis=0, keepdims=True)


def assemble(dst, pieces, q):
    n = pieces[0].shape[0]
    for k in range(3):
        dst[pl.ds(pl.multiple_of((q ^ k) * n, 16), n), :] = pieces[k][...]
    last = pl.multiple_of((q ^ 3) * n, 16)
    dst[pl.ds(last, n // 2), :] = pieces[3][...]
    dst[pl.ds(pl.multiple_of(last + n // 2, 16), n // 2), :] = pieces[4][...]


def attn_forward(first, save, meta, *refs):
    refs = list(refs)
    if first:
        x_in = refs.pop(0)
    else:
        base, mine, theirs, gain_prev, shift_prev = [refs.pop(0) for _ in range(5)]
    own = refs.pop(0)
    pieces = [refs.pop(0) for _ in range(5)]
    bias, shift = [refs.pop(0) for _ in range(2)]
    base_out, part_out = [refs.pop(0) for _ in range(2)]
    if save:
        hidden_out, proj_out, probs_out, mixed_out = [refs.pop(0) for _ in range(4)]
        if not first:
            xhat_out, rate_out = [refs.pop(0) for _ in range(2)]
    far = refs.pop(0)
    crop = pl.program_id(0)

    @pl.when(crop == 0)
    def _():
        assemble(far, pieces, meta[0])

    if first:
        low = x_in[...]
        x = low.astype(F32)
    else:
        v = base[...] + (mine[...].astype(F32) + theirs[...].astype(F32))
        xhat, rate, x = norm(v, gain_prev[1:2, :], shift_prev[3:4, :])
        low = x.astype(BF)
        if save:
            xhat_out[...] = xhat
            rate_out[...] = rate
    width = bias.shape[1] // 3
    heads = width // HEAD
    visible = lax.broadcasted_iota(jnp.int32, (1, SEQ), 1) < meta[1 + crop]
    total = None
    for s, w in enumerate((own, far)):
        proj = (mm_nt(low, w[: 3 * width, :]) + bias[s : s + 1, :]).astype(BF)
        mixed = []
        for h in range(heads):
            queries = proj[:, h * HEAD : (h + 1) * HEAD]
            keys = proj[:, width + h * HEAD : width + (h + 1) * HEAD]
            values = proj[:, 2 * width + h * HEAD : 2 * width + (h + 1) * HEAD]
            scores = jnp.where(visible, mm_nt(queries, keys) * SCALE, FILL)
            e = jnp.exp(scores - jnp.max(scores, axis=1, keepdims=True))
            probs = (e * (1.0 / jnp.sum(e, axis=1, keepdims=True))).astype(BF)
            if save:
                probs_out[s, 0, h] = probs
            mixed.append(mm(probs, values).astype(BF))
        mixed = jnp.concatenate(mixed, axis=1)
        if save:
            proj_out[s] = proj
            mixed_out[s] = mixed
        term = mm(mixed, w[3 * width : 4 * width, :])
        total = term if total is None else total + term
    if save:
        hidden_out[...] = low
    base_out[...] = x + shift[0:1, :]
    part_out[...] = total.astype(BF)


def ffn_forward(save, meta, *refs):
    refs = list(refs)
    base, mine, theirs, own_in, own_down = [refs.pop(0) for _ in range(5)]
    pieces_in = [refs.pop(0) for _ in range(5)]
    pieces_down = [refs.pop(0) for _ in range(5)]
    bias, gain, shift = [refs.pop(0) for _ in range(3)]
    base_out, part_out = [refs.pop(0) for _ in range(2)]
    if save:
        xhat_out, rate_out, normed_out, active_out, slope_out = [refs.pop(0) for _ in range(5)]
    far_in, far_down = refs

    @pl.when(pl.program_id(0) == 0)
    def _():
        assemble(far_in, pieces_in, meta[0])
        assemble(far_down, pieces_down, meta[0])

    v = base[...] + (mine[...].astype(F32) + theirs[...].astype(F32))
    xhat, rate, normed = norm(v, gain[0:1, :], shift[1:2, :])
    low = normed.astype(BF)
    if save:
        xhat_out[...] = xhat
        rate_out[...] = rate
        normed_out[...] = low
    total = None
    for s, (w_in, w_down) in enumerate(((own_in, own_down), (far_in, far_down))):
        u = mm(low, w_in[...]) + bias[s : s + 1, :]
        share = 0.5 + 0.5 * lax.erf(u * (0.5**0.5))
        active = (u * share).astype(BF)
        if save:
            active_out[s] = active
            slope_out[s] = (share + u * (jnp.exp(-0.5 * u * u) * ((2 * math.pi) ** -0.5))).astype(BF)
        term = mm(active, w_down[...])
        total = term if total is None else total + term
    base_out[...] = normed + shift[2:3, :]
    part_out[...] = total.astype(BF)


def pool_forward(save, meta, base, mine, theirs, gain, shift, sums_out, *saved):
    crop = pl.program_id(0)
    v = base[...] + (mine[...].astype(F32) + theirs[...].astype(F32))
    xhat, rate, x = norm(v, gain[1:2, :], shift[3:4, :])
    if save:
        saved[0][...] = xhat
        saved[1][...] = rate
    visible = lax.broadcasted_iota(jnp.int32, (SEQ, 1), 0) < meta[1 + crop]
    sums_out[0] = rows(jnp.where(visible, x, 0.0))


def flips(dp_size, with_core):
    d = lax.axis_index("dp")
    t = lax.axis_index("tensor")
    found = [(d, t ^ 2)]
    for b in range(dp_size.bit_length() - 1):
        found.append((d ^ (1 << b), t))
    if with_core:
        found.append((d, t ^ 1))
    return found


def greet(partners):
    barrier = pltpu.get_barrier_semaphore()
    for p in partners:
        pl.semaphore_signal(barrier, inc=1, device_id=p, device_id_type=MESH)
    pl.semaphore_wait(barrier, len(partners))


def contrast(dp_size, nc, count, inv_q, inv_k, sums_q, sums_k, pair_out, grad_out, held, send, recv):
    wide = D + 128
    d = lax.axis_index("dp")
    half = lax.axis_index("tensor") // 2
    me = d * 2 + half
    partners = flips(dp_size, False)
    greet(partners)

    def unit(s, inv):
        pooled = s * inv
        r = lax.rsqrt(jnp.sum(pooled * pooled, axis=1, keepdims=True) + EPS)
        return pooled * r, r

    unit_q, rate_q = unit(sums_q[...], inv_q[...])
    unit_k, _ = unit(sums_k[...], inv_k[...])
    held[me] = jnp.zeros((8, wide), F32)
    held[me, 0:nc, 0:D] = unit_k
    held[me, nc : 2 * nc, 0:D] = unit_q
    slot = half * nc + lax.broadcasted_iota(jnp.int32, (nc, 128), 0)
    lane = lax.broadcasted_iota(jnp.int32, (nc, 128), 1)
    held[me, 0:nc, D:wide] = jnp.where((slot < count[0]) & (lane == 0), 1.0, 0.0)
    for s, p in enumerate(partners):
        block = pl.ds(((me >> s) << s), 1 << s)
        copy = pltpu.make_async_remote_copy(
            src_ref=held.at[block],
            dst_ref=held.at[block],
            send_sem=send.at[s],
            recv_sem=recv.at[s],
            device_id=p,
            device_id_type=MESH,
        )
        copy.start()
        copy.wait()
    chips = held.shape[0]
    every = held[...].reshape(chips * 8, wide)
    keys = every[:, 0:D]
    here = held[pl.ds(2 * d, 2)].reshape(16, wide)[:, 0:D]

    def exact(a, b, dims):
        return lax.dot_general(
            a, b, (dims, ((), ())), precision=lax.Precision.HIGHEST, preferred_element_type=F32
        )

    one = jnp.where(lax.broadcasted_iota(jnp.int32, (16, 128), 1) == 0, 1.0, 0.0)
    live = exact(one, every[:, D:wide], ((1,), (1,))) > 0.5
    logits = exact(here, keys, ((1,), (1,))) / TEMPER
    masked = jnp.where(live, logits, FILL)
    highest = jnp.max(masked, axis=1, keepdims=True)
    e = jnp.exp(masked - highest)
    total = jnp.sum(e, axis=1, keepdims=True)
    row = lax.broadcasted_iota(jnp.int32, (16, 1), 0)
    chip = row // 8
    place = row % 8 - nc
    column = lax.broadcasted_iota(jnp.int32, (16, chips * 8), 1)
    own = column == (2 * d + chip) * 8 + place
    mine = (place >= 0) & (place < nc) & (chip * nc + place < count[0])
    own_logit = jnp.sum(jnp.where(own, logits, 0.0), axis=1, keepdims=True)
    pair_out[...] = jnp.broadcast_to(
        jnp.where(mine, highest + jnp.log(total) - own_logit, 0.0), (16, 128)
    )
    weighting = jnp.where(mine, e / total - own.astype(F32), 0.0) * (SEQ / TEMPER)
    g_unit = exact(weighting, keys, ((1,), (0,)))
    mine_first = half == 0
    g_unit = jnp.where(mine_first, g_unit[nc : 2 * nc], g_unit[8 + nc : 8 + 2 * nc])
    g_pooled = rate_q * (g_unit - unit_q * jnp.sum(unit_q * g_unit, axis=1, keepdims=True))
    grad_out[...] = g_pooled * inv_q[...]


def total_over(dp_size, v_ref, out_ref, held, got, send, recv):
    partners = flips(dp_size, True)
    greet(partners)
    held[0] = v_ref[...]
    for s, p in enumerate(partners):
        copy = pltpu.make_async_remote_copy(
            src_ref=held.at[s],
            dst_ref=got.at[s],
            send_sem=send.at[s],
            recv_sem=recv.at[s],
            device_id=p,
            device_id_type=MESH,
        )
        copy.start()
        copy.wait()
        held[s + 1] = held[s] + got[s]
    out_ref[...] = held[len(partners)]


def ffn_backward(top, meta, *refs):
    refs = list(refs)
    if top:
        g_sum = refs.pop(0)
    else:
        base, theirs = [refs.pop(0) for _ in range(2)]
    xhat, rate, slope, own_in, own_down = [refs.pop(0) for _ in range(5)]
    pieces_in = [refs.pop(0) for _ in range(5)]
    pieces_down = [refs.pop(0) for _ in range(5)]
    gain = refs.pop(0)
    base_out, part_out, low_out, inner_out, vec_out, bias_out = [refs.pop(0) for _ in range(6)]
    far_in, far_down = refs
    crop = pl.program_id(0)

    @pl.when(crop == 0)
    def _():
        assemble(far_in, pieces_in, meta[0])
        assemble(far_down, pieces_down, meta[0])
        vec_out[...] = jnp.zeros_like(vec_out)
        bias_out[...] = jnp.zeros_like(bias_out)

    if top:
        visible = lax.broadcasted_iota(jnp.int32, (SEQ, 1), 0) < meta[1 + crop]
        g = jnp.where(visible, g_sum[0], 0.0)
    else:
        g = base[...] + theirs[...].astype(F32)
    xh = xhat[...]
    gc = norm_back(g, xh, rate[...], gain[1:2, :])
    vec_out[0:1, :] += rows(g * xh)
    vec_out[1:2, :] += rows(g)
    vec_out[2:3, :] += rows(gc)
    low = gc.astype(BF)
    low_out[...] = low
    total = gc
    part = None
    for s, (w_in, w_down) in enumerate(((own_in, own_down), (far_in, far_down))):
        inner = (mm_nt(low, w_down[...]) * slope[s].astype(F32)).astype(BF)
        inner_out[s] = inner
        bias_out[s : s + 1, :] += rows(inner.astype(F32))
        term = mm_nt(inner, w_in[...])
        part = term if part is None else part + term
    base_out[...] = total + part
    part_out[...] = part.astype(BF)


def attn_backward(meta, *refs):
    refs = list(refs)
    base, theirs, xhat, rate, proj, probs, own = [refs.pop(0) for _ in range(7)]
    pieces = [refs.pop(0) for _ in range(5)]
    gain = refs.pop(0)
    base_out, part_out, low_out, proj_out, vec_out, bias_out = [refs.pop(0) for _ in range(6)]
    far = refs.pop(0)
    crop = pl.program_id(0)

    @pl.when(crop == 0)
    def _():
        assemble(far, pieces, meta[0])
        vec_out[...] = jnp.zeros_like(vec_out)
        bias_out[...] = jnp.zeros_like(bias_out)

    g = base[...] + theirs[...].astype(F32)
    xh = xhat[...]
    gr = norm_back(g, xh, rate[...], gain[0:1, :])
    vec_out[0:1, :] += rows(g * xh)
    vec_out[1:2, :] += rows(g)
    vec_out[2:3, :] += rows(gr)
    low = gr.astype(BF)
    low_out[...] = low
    width = proj.shape[2] // 3
    heads = width // HEAD
    part = None
    for s, w in enumerate((own, far)):
        g_mixed = mm_nt(low, w[3 * width : 4 * width, :]).astype(BF)
        pr = proj[s]
        parts = [[], [], []]
        for h in range(heads):
            queries = pr[:, h * HEAD : (h + 1) * HEAD]
            keys = pr[:, width + h * HEAD : width + (h + 1) * HEAD]
            values = pr[:, 2 * width + h * HEAD : 2 * width + (h + 1) * HEAD]
            gm = g_mixed[:, h * HEAD : (h + 1) * HEAD]
            p_low = probs[s, 0, h]
            p = p_low.astype(F32)
            gp = mm_nt(gm, values)
            gs = (p * (gp - jnp.sum(p * gp, axis=1, keepdims=True))).astype(BF)
            parts[0].append((mm(gs, keys) * SCALE).astype(BF))
            parts[1].append((mm_tn(gs, queries) * SCALE).astype(BF))
            parts[2].append(mm_tn(p_low, gm).astype(BF))
        g_proj = jnp.concatenate(parts[0] + parts[1] + parts[2], axis=1)
        proj_out[s] = g_proj
        bias_out[s : s + 1, :] += rows(g_proj.astype(F32))
        term = mm(g_proj, w[: 3 * width, :])
        part = term if part is None else part + term
    base_out[...] = gr + part
    part_out[...] = part.astype(BF)


def ffn_weights(low, active, normed, inner, in_out, down_out):
    down_out[0] = mm_tn(low[...], active[0])
    in_out[0] = mm_tn(normed[...], inner[0])


def attn_weights(low, mixed, hidden, g_proj, out):
    width = mixed.shape[2]
    out[0, :, 0 : 3 * width] = mm_tn(hidden[...], g_proj[0])
    out[0, :, 3 * width : 4 * width] = mm_tn(low[...], mixed[0])


SMEM = pl.BlockSpec(memory_space=pltpu.SMEM)


def row_block(width):
    return pl.BlockSpec((SEQ, width), lambda i: (i, 0))


def shard_block(width):
    return pl.BlockSpec((2, SEQ, width), lambda i: (0, i, 0))


def whole_block(shape):
    return pl.BlockSpec(shape, lambda i: (0,) * len(shape))


def call(body, grid, ins, outs, scratch, flops, name):
    arrays = [a for a, _ in ins]
    size = sum(a.size * a.dtype.itemsize for a in arrays)
    size += sum(math.prod(s) * jnp.dtype(t).itemsize for s, t, _ in outs)
    return pl.pallas_call(
        body,
        grid=grid,
        in_specs=[s for _, s in ins],
        out_specs=[s for _, _, s in outs],
        out_shape=[jax.ShapeDtypeStruct(s, t) for s, t, _ in outs],
        scratch_shapes=scratch,
        compiler_params=pltpu.CompilerParams(vmem_limit_bytes=52 * MIB),
        cost_estimate=pl.CostEstimate(flops=int(flops), bytes_accessed=int(size), transcendentals=0),
        name=name,
    )(*arrays)


def on_device(mesh_shape, *args):
    (
        query_input,
        key_input,
        query_length,
        key_length,
        pair_count,
    ) = args[:5]
    encoders = (args[5:13], args[13:21])
    dp_size = mesh_shape["dp"]
    dp_bits = dp_size.bit_length() - 1
    d_pos = lax.axis_index("dp")
    t_pos = lax.axis_index("tensor")
    quarter = d_pos & 3
    core = t_pos & 1
    half = t_pos // 2
    share = query_input.shape[0]
    total_rows = 2 * share
    nc = total_rows // SEQ
    width = args[5].shape[3]

    def far_perm(x):
        return lax.ppermute(x, "tensor", [(i, i ^ 2) for i in range(4)])

    def core_perm(x):
        return lax.ppermute(x, "tensor", [(i, i ^ 1) for i in range(4)])

    def dp_perm(x, bit):
        return lax.ppermute(x, "dp", [(i, i ^ (1 << bit)) for i in range(dp_size)])

    def fetch(blob):
        n = blob.shape[0] // 4
        r0 = far_perm(lax.dynamic_slice(blob, (quarter * n, 0), (n, blob.shape[1])))
        r1 = dp_perm(r0, 0)
        r2 = dp_perm(r0, 1)
        r3 = dp_perm(r2[: n // 2], 0)
        r4 = dp_perm(r1[n // 2 :], 1)
        return (r0, r1, r2, r3, r4)

    def chip_rows(x):
        other = core_perm(x)
        return jnp.where(core == 0, jnp.concatenate([x, other]), jnp.concatenate([other, x]))

    small = jnp.stack(
        [jnp.concatenate([w[1].reshape(-1), w[4].reshape(-1)]) for w in encoders]
    )
    small_far = far_perm(small)
    own = [[None] * LAYERS for _ in range(2)]
    far = [[None] * LAYERS for _ in range(2)]
    qkv_bias = [[None] * LAYERS for _ in range(2)]
    in_bias = [[None] * LAYERS for _ in range(2)]
    for layer in range(LAYERS):
        for e, w in enumerate(encoders):
            attn = jnp.concatenate(
                [w[0][layer].transpose(1, 2, 0).reshape(3 * width, D), w[2][layer]], axis=0
            )
            own[e][layer] = (attn, w[3][layer], w[5][layer])
            far[e][layer] = tuple(fetch(b) for b in own[e][layer])
            pair = []
            inner_rows = []
            for v in (small, small_far):
                qv = v[e, : LAYERS * 2 * width].reshape(LAYERS, 2, width)[layer]
                pair.append(jnp.concatenate([qv[0], jnp.zeros((width,), F32), qv[1]]))
                inner_rows.append(v[e, LAYERS * 2 * width :].reshape(LAYERS, -1)[layer])
            qkv_bias[e][layer] = jnp.stack(pair)
            in_bias[e][layer] = jnp.stack(inner_rows)

    lengths = [
        lax.dynamic_slice(v, (half * nc,), (nc,)) for v in (query_length, key_length)
    ]
    metas = [jnp.concatenate([quarter[None], v]).astype(jnp.int32) for v in lengths]
    grid = (nc,)
    wspec = whole_block((BLOB, D))
    pspecs = [whole_block((BLOB // 4, D))] * 3 + [whole_block((BLOB // 8, D))] * 2
    gspec = whole_block((2, D))
    sspec = whole_block((4, D))
    flat = row_block(D)
    blob_scratch = pltpu.VMEM((BLOB, D), BF)
    big = (total_rows, D)
    unit_flops = 2 * total_rows * D

    def weight_ins(e, layer, which):
        return [(own[e][layer][which], wspec)]

    def piece_ins(e, layer, which):
        return list(zip(far[e][layer][which], pspecs))

    state = [None, None]
    kept = [dict() for _ in range(LAYERS)]
    x_in = [chip_rows(query_input), chip_rows(key_input)]
    for layer in range(LAYERS):
        for e in range(2):
            save = e == 0
            gains, shifts = encoders[e][6], encoders[e][7]
            ins = [(metas[e], SMEM)]
            if layer == 0:
                ins += [(x_in[e], flat)]
            else:
                ins += [(a, flat) for a in state[e]]
                ins += [(gains[layer - 1], gspec), (shifts[layer - 1], sspec)]
            ins += weight_ins(e, layer, 0) + piece_ins(e, layer, 0)
            ins += [(qkv_bias[e][layer], whole_block((2, 3 * width))), (shifts[layer], sspec)]
            outs = [(big, F32, flat), (big, BF, flat)]
            if save:
                heads = width // HEAD
                outs += [
                    (big, BF, flat),
                    ((2, total_rows, 3 * width), BF, shard_block(3 * width)),
                    (
                        (2, nc, heads, SEQ, SEQ),
                        BF,
                        pl.BlockSpec((2, 1, heads, SEQ, SEQ), lambda i: (0, i, 0, 0, 0)),
                    ),
                    ((2, total_rows, width), BF, shard_block(width)),
                ]
                if layer > 0:
                    outs += [(big, F32, flat), ((total_rows, 1), F32, row_block(1))]
            got = call(
                functools.partial(attn_forward, layer == 0, save),
                grid,
                ins,
                outs,
                [blob_scratch],
                unit_flops * 10 * width,
                f"attn_forward_{e}_{layer}",
            )
            base, part = got[:2]
            if save:
                kept[layer].update(zip(("hidden", "proj", "probs", "mixed"), got[2:6]))
                if layer > 0:
                    kept[layer - 1].update(zip(("xhat2", "rate2"), got[6:8]))
            other = core_perm(part)
            ins = [(metas[e], SMEM), (base, flat), (part, flat), (other, flat)]
            ins += weight_ins(e, layer, 1) + weight_ins(e, layer, 2)
            ins += piece_ins(e, layer, 1) + piece_ins(e, layer, 2)
            ins += [(in_bias[e][layer], whole_block((2, BLOB))), (gains[layer], gspec), (shifts[layer], sspec)]
            outs = [(big, F32, flat), (big, BF, flat)]
            if save:
                outs += [
                    (big, F32, flat),
                    ((total_rows, 1), F32, row_block(1)),
                    (big, BF, flat),
                    ((2, total_rows, BLOB), BF, shard_block(BLOB)),
                    ((2, total_rows, BLOB), BF, shard_block(BLOB)),
                ]
            got = call(
                functools.partial(ffn_forward, save),
                grid,
                ins,
                outs,
                [blob_scratch, blob_scratch],
                unit_flops * 4 * BLOB,
                f"ffn_forward_{e}_{layer}",
            )
            if save:
                kept[layer].update(
                    zip(("xhat1", "rate1", "normed", "active", "slope"), got[2:7])
                )
            state[e] = (got[0], got[1], core_perm(got[1]))
    sums = []
    for e in range(2):
        save = e == 0
        gains, shifts = encoders[e][6], encoders[e][7]
        outs = [((nc, 1, D), F32, pl.BlockSpec((1, 1, D), lambda i: (i, 0, 0)))]
        if save:
            outs += [(big, F32, flat), ((total_rows, 1), F32, row_block(1))]
        got = call(
            functools.partial(pool_forward, save),
            grid,
            [(metas[e], SMEM)]
            + [(a, flat) for a in state[e]]
            + [(gains[LAYERS - 1], gspec), (shifts[LAYERS - 1], sspec)],
            outs,
            [],
            unit_flops,
            f"pool_forward_{e}",
        )
        sums.append(got[0].reshape(nc, D))
        if save:
            kept[LAYERS - 1].update(zip(("xhat2", "rate2"), got[1:3]))

    inverse = [(1.0 / v.astype(F32))[:, None] for v in lengths]
    vmem = pl.BlockSpec(memory_space=pltpu.VMEM)
    hops = dp_bits + 1
    pair_rows, g_sum = pl.pallas_call(
        functools.partial(contrast, dp_size, nc),
        in_specs=[SMEM] + [vmem] * 4,
        out_specs=[vmem] * 2,
        out_shape=[
            jax.ShapeDtypeStruct((16, 128), F32),
            jax.ShapeDtypeStruct((nc, D), F32),
        ],
        scratch_shapes=[
            pltpu.VMEM((2 * dp_size, 8, D + 128), F32),
            pltpu.SemaphoreType.DMA((hops,)),
            pltpu.SemaphoreType.DMA((hops,)),
        ],
        compiler_params=pltpu.CompilerParams(
            collective_id=0, has_side_effects=True, vmem_limit_bytes=40 * MIB
        ),
        name="contrast",
    )(pair_count, inverse[0], inverse[1], sums[0], sums[1])
    per_pair = jnp.concatenate([pair_rows[nc : 2 * nc, 0], pair_rows[8 + nc : 8 + 2 * nc, 0]])

    def scatter(full, order):
        cur = full.reshape((2,) + (2,) * dp_bits + (D // dp_size, BLOB))
        axes = ["y"] + list(reversed(range(dp_bits)))
        for name in order:
            at = axes.index(name)
            bit = jnp.int32(0) if name == "y" else (d_pos >> name) & 1
            keep = lax.dynamic_index_in_dim(cur, bit, at, keepdims=False)
            send = lax.dynamic_index_in_dim(cur, 1 - bit, at, keepdims=False)
            got = far_perm(send) if name == "y" else dp_perm(send, name)
            cur = keep + got
            axes.pop(at)
        return cur

    rest = list(range(2, dp_bits))
    order_in = ["y", 0, 1] + rest
    order_down = [0, "y", 1] + rest
    order_attn = [1, "y", 0] + rest

    vec_spec = whole_block((8, D))
    grad_in = [None] * LAYERS
    grad_down = [None] * LAYERS
    grad_attn = [None] * LAYERS
    vectors = [None] * LAYERS
    g_state = None
    for layer in reversed(range(LAYERS)):
        w = encoders[0]
        gains = w[6]
        k = kept[layer]
        top = layer == LAYERS - 1
        ins = [(metas[0], SMEM)]
        if top:
            ins += [(g_sum.reshape(nc, 1, D), pl.BlockSpec((1, 1, D), lambda i: (i, 0, 0)))]
        else:
            ins += [(a, flat) for a in g_state]
        ins += [(k["xhat2"], flat), (k["rate2"], row_block(1)), (k["slope"], shard_block(BLOB))]
        ins += weight_ins(0, layer, 1) + weight_ins(0, layer, 2)
        ins += piece_ins(0, layer, 1) + piece_ins(0, layer, 2)
        ins += [(gains[layer], gspec)]
        base, part, low, inner, vec_f, bias_f = call(
            functools.partial(ffn_backward, top),
            grid,
            ins,
            [
                (big, F32, flat),
                (big, BF, flat),
                (big, BF, flat),
                ((2, total_rows, BLOB), BF, shard_block(BLOB)),
                ((8, D), F32, vec_spec),
                ((8, BLOB), F32, whole_block((8, BLOB))),
            ],
            [blob_scratch, blob_scratch],
            unit_flops * 4 * BLOB,
            f"ffn_backward_{layer}",
        )
        other = core_perm(part)
        one_shard = pl.BlockSpec((1, total_rows, BLOB), lambda i: (i, 0, 0))
        full_out = pl.BlockSpec((1, D, BLOB), lambda i: (i, 0, 0))
        g_in, g_down = call(
            ffn_weights,
            (2,),
            [
                (low, whole_block(big)),
                (k["active"], one_shard),
                (k["normed"], whole_block(big)),
                (inner, one_shard),
            ],
            [((2, D, BLOB), F32, full_out), ((2, D, BLOB), F32, full_out)],
            [],
            unit_flops * 4 * BLOB,
            f"ffn_weights_{layer}",
        )
        grad_in[layer] = scatter(g_in, order_in)
        grad_down[layer] = scatter(g_down, order_down)
        ins = [(metas[0], SMEM), (base, flat), (other, flat)]
        ins += [(k["xhat1"], flat), (k["rate1"], row_block(1)), (k["proj"], shard_block(3 * width))]
        heads = width // HEAD
        ins += [(k["probs"], pl.BlockSpec((2, 1, heads, SEQ, SEQ), lambda i: (0, i, 0, 0, 0)))]
        ins += weight_ins(0, layer, 0) + piece_ins(0, layer, 0)
        ins += [(gains[layer], gspec)]
        base, part, low, g_proj, vec_a, bias_a = call(
            attn_backward,
            grid,
            ins,
            [
                (big, F32, flat),
                (big, BF, flat),
                (big, BF, flat),
                ((2, total_rows, 3 * width), BF, shard_block(3 * width)),
                ((8, D), F32, vec_spec),
                ((8, 3 * width), F32, whole_block((8, 3 * width))),
            ],
            [blob_scratch],
            unit_flops * 14 * width,
            f"attn_backward_{layer}",
        )
        if layer > 0:
            g_state = (base, core_perm(part))
        else:
            mine = lax.dynamic_slice(base, (core * share, 0), (share, D))
            away = lax.dynamic_slice(part, ((1 - core) * share, 0), (share, D))
            query_grad = mine + core_perm(away).astype(F32)
        (g_attn,) = call(
            attn_weights,
            (2,),
            [
                (low, whole_block(big)),
                (k["mixed"], pl.BlockSpec((1, total_rows, width), lambda i: (i, 0, 0))),
                (k["hidden"], whole_block(big)),
                (g_proj, pl.BlockSpec((1, total_rows, 3 * width), lambda i: (i, 0, 0))),
            ],
            [((2, D, BLOB), F32, full_out)],
            [],
            unit_flops * 8 * width,
            f"attn_weights_{layer}",
        )
        grad_attn[layer] = scatter(g_attn, order_attn)
        vectors[layer] = (vec_f, bias_f, vec_a, bias_a)

    first = jnp.where(core == 0, 1.0, 0.0)
    packed = []
    for vec_f, bias_f, vec_a, bias_a in vectors:
        norms = jnp.stack([vec_a[0], vec_f[0], vec_a[2], vec_a[1], vec_f[2], vec_f[1]]) * first
        inner_rows = jnp.zeros((4, BLOB), F32)
        inner_rows = lax.dynamic_update_slice(inner_rows, bias_f[0:1], (t_pos, 0))
        inner_rows = lax.dynamic_update_slice(inner_rows, bias_f[1:2], (t_pos ^ 2, 0))
        qv = jnp.zeros((4, 2, width), F32)
        for s, at in ((0, t_pos), (1, t_pos ^ 2)):
            both = jnp.stack([bias_a[s, :width], bias_a[s, 2 * width :]])
            qv = lax.dynamic_update_slice(qv, both[None], (at, 0, 0))
        packed.append(jnp.concatenate([norms, inner_rows, qv.transpose(1, 0, 2).reshape(2, 4 * width)]))
    packed = jnp.concatenate(packed)
    hops += 1
    summed = pl.pallas_call(
        functools.partial(total_over, dp_size),
        in_specs=[vmem],
        out_specs=vmem,
        out_shape=jax.ShapeDtypeStruct(packed.shape, F32),
        scratch_shapes=[
            pltpu.VMEM((hops + 1,) + packed.shape, F32),
            pltpu.VMEM((hops,) + packed.shape, F32),
            pltpu.SemaphoreType.DMA((hops,)),
            pltpu.SemaphoreType.DMA((hops,)),
        ],
        compiler_params=pltpu.CompilerParams(
            collective_id=1, has_side_effects=True, vmem_limit_bytes=16 * MIB
        ),
        name="total_over",
    )(packed)
    summed = summed.reshape(LAYERS, 12, D)
    grad_gain = summed[:, 0:2]
    grad_shift = summed[:, 2:6]
    grad_in_bias = summed[:, 6:10].reshape(LAYERS, 4 * BLOB)
    grad_qv_bias = summed[:, 10:12]

    attn = jnp.stack(grad_attn)
    return (
        per_pair,
        query_grad,
        attn[:, :, : 3 * width].reshape(LAYERS, D // dp_size, 3, width),
        attn[:, :, 3 * width :].transpose(0, 2, 1),
        jnp.stack(grad_in),
        jnp.stack(grad_down).transpose(0, 2, 1),
        grad_qv_bias,
        grad_in_bias,
        grad_gain,
        grad_shift,
    )


def solution(mesh):
    split = P(("dp", "tensor"), None)
    weights = (
        P(None, None, None, "tensor"),
        P(None, None, "tensor"),
        P(None, "tensor", None),
        P(None, None, "tensor"),
        P(None, "tensor"),
        P(None, "tensor", None),
        P(),
        P(),
    )
    return jax.shard_map(
        functools.partial(on_device, dict(mesh.shape)),
        mesh=mesh,
        in_specs=(split, split, P("dp"), P("dp"), P("dp")) + weights + weights,
        out_specs=(
            P("dp"),
            split,
            P(None, "dp", None, "tensor"),
            P(None, "tensor", "dp"),
            P(None, "dp", "tensor"),
            P(None, "tensor", "dp"),
            P(),
            P(),
            P(),
            P(),
        ),
        check_vma=False,
    )
```

time: 1710 us -> 659 us (0.39)
  waiting for transfers between devices: 1260 us -> 178 us
  Pallas kernels: 0 us -> 265 us
  matrix products: 198 us -> 0 us
  starting transfers between devices: 3.9 us -> 89.5 us
  blocking collectives: 46.1 us -> 0 us
  other arithmetic: 75.6 us -> 41.3 us
  local copies, waits for them, and re-layouts: 94.2 us -> 71.4 us
    reduce_scatter x13 -> x0, waiting for transfers between devices: 620 us -> none  [the longest x4 168 us: forward_layer(): lax.psum_scatter(matmul_plain(mixed, out_layer), 'tensor', scatter_dimens...]
    pallas_call x0 -> x20, Pallas kernels: none -> 265 us  [the longest x18 182 us: call(): pl.pallas_call(body, grid=grid, in_specs=[s for _, s in ins], out_specs=[...]
    all_gather x12 -> x0, waiting for transfers between devices: 257 us -> none  [the longest x4 91.2 us: forward_layer(): lax.all_gather(x_share.astype(jnp.bfloat16), 'tensor', axis=0, tiled=True)]
    unnamed x32 -> x0, waiting for transfers between devices: 257 us -> none
    dot_general x51 -> x0, matrix products: 198 us -> none  [the longest x14 104 us: matmul_plain(): return jnp.dot(left, right, preferred_element_type=jnp.float32)]
    ppermute x0 -> x99, waiting for transfers between devices: none -> 178 us  [the longest x66 152 us: dp_perm(): return lax.ppermute(x, 'dp', [(i, i ^ 1 << bit) for i in range(dp_size)])]
    psum x1 -> x0, waiting for transfers between devices: 128 us -> none  [on_device(): lax.psum((qv_full, in_full, gain_stack, shift_stack), ('dp', 'tensor'))]
    ppermute x0 -> x99, starting transfers between devices: none -> 89.5 us  [the longest x66 49.6 us: dp_perm(): return lax.ppermute(x, 'dp', [(i, i ^ 1 << bit) for i in range(dp_size)])]
  transfers between devices with their start and end apart: 29 -> 99, of which waited for: 29 -> 29; matrix products, arithmetic and copies ran while one was open for 9% -> 15% of each run, Pallas kernels for 0% -> 35%
where the time goes in v1:
time: 659 us; the launch traced here: 648 us
  Pallas kernels  265 us (40%)
  waiting for transfers between devices  178 us (27%)
  starting transfers between devices  89.5 us (14%)
  local copies, waits for them, and re-layouts  71.4 us (11%)
  other arithmetic  41.3 us (6%)
    pallas_call x18, Pallas kernels, call(): pl.pallas_call(body, grid=grid, in_specs=[s for _, s in ins], out_specs=[...  182 us
    ppermute x66, waiting for transfers between devices, dp_perm(): return lax.ppermute(x, 'dp', [(i, i ^ 1 << bit) for i in range(dp_size)])  152 us
    pallas_call x1, Pallas kernels, on_device(): pl.pallas_call(functools.partial(total_over, dp_size), in_specs=[vmem], o...  63.2 us
    ppermute x66, starting transfers between devices, dp_perm(): return lax.ppermute(x, 'dp', [(i, i ^ 1 << bit) for i in range(dp_size)])  49.6 us
    ppermute x19, waiting for transfers between devices, far_perm(): return lax.ppermute(x, 'tensor', [(i, i ^ 2) for i in range(4)])  25.5 us
    ppermute x14, starting transfers between devices, core_perm(): return lax.ppermute(x, 'tensor', [(i, i ^ 1) for i in range(4)])  23.7 us
    add x18, other arithmetic, scatter(): cur = keep + got  20.7 us
    pallas_call x1, Pallas kernels, on_device(): pl.pallas_call(functools.partial(contrast, dp_size, nc), in_specs=[SMEM]...  19.9 us
  transfers between devices with their start and end apart: 99, of which 29 were waited for; matrix products, arithmetic and copies ran while one was open for 15% of the time, Pallas kernels for 35%

profile of v1, /device:TPU:29, one launch (start us, length us, event | category | flops | bytes accessed | tf_op | source)
XLA Modules:
  0.0 648.5 jit_solution(12249296400328986846)
XLA Ops:
  39.1 6.1 collective-permute-done.8.refs_5_.refs_7_
  61.4 11.3 %attn_forward_1_0.1 = (f32[768,768]{1,0:T(8,128)}, bf16[768,768]{1,0:T(8,128)(2,1)}) custom-call(s32[4]{0:T(128)S(1)} %pad_add_fusion.1.meta, bf16[768,768]{1,0:T(8,128)(2,1)} %maximum_select_fusion.1.refs_0_, bf16[768,768]{1,0:T(8,128)(2,1)} %pad_maximum_fusion.2.refs_1_, bf16[192,768]{1,0:T(8,128)(2,1)S(1)} %collective-permute-done.37.refs_2_, ...), custom_call_target="tpu_custom_call" | custom-call | flops 2264924160 | bytes 7094800 | tf_op jit(solution)/shard_map/attn_forward_1_0/pallas_call | solution.py:406
  79.0 12.0 %attn_forward_0_0.1 = (f32[768,768]{1,0:T(8,128)}, bf16[768,768]{1,0:T(8,128)(2,1)}, bf16[768,768]{1,0:T(8,128)(2,1)}, bf16[2,768,576]{2,1,0:T(8,128)(2,1)}, bf1...) custom-call(s32[4]{0:T(128)S(1)} %pad_add_fusion.meta, bf16[768,768]{1,0:T(8,128)(2,1)} %maximum_select_fusion.refs_0_, ...), custom_call_target="tpu_custom_call" | custom-call | flops 2264924160 | bytes 12993040 | tf_op jit(solution)/shard_map/attn_forward_0_0/pallas_call | solution.py:406
  95.2 5.5 collective-permute-done.15.refs_12_.refs_14_
  110.4 9.5 %ffn_forward_1_0.1 = (f32[768,768]{1,0:T(8,128)}, bf16[768,768]{1,0:T(8,128)(2,1)}) custom-call(s32[4]{0:T(128)S(1)} %pad_add_fusion.1.meta, f32[768,768]{1,0:T(8,128)} %get-tuple-element.88.refs_0_, bf16[768,768]{1,0:T(8,128)(2,1)} %get-tuple-element.89.refs_1_, bf16[768,768]{1,0:T(8,128)(2,1)} %copy-done.98, bf16[768,768]{1,0:T(8,128)(2,1)} %get-tuple-element.193.refs_3_, ...), custom_call_target="tpu_custom_call" | custom-call | flops 3623878656 | bytes 13000720 | tf_op jit(solution)/shard_map/ffn_forward_1_0/pallas_call | solution.py:406
  128.6 11.1 %ffn_forward_0_0.1 = (f32[768,768]{1,0:T(8,128)}, bf16[768,768]{1,0:T(8,128)(2,1)}, f32[768,768]{1,0:T(8,128)}, f32[768,1]{1,0:T(8,128)}, bf16[768,768]{1,0:T(8,...) custom-call(s32[4]{0:T(128)S(1)} %pad_add_fusion.meta, f32[768,768]{1,0:T(8,128)} %get-tuple-element.79.refs_0_, ...), custom_call_target="tpu_custom_call" | custom-call | flops 3623878656 | bytes 21261328 | tf_op jit(solution)/shard_map/ffn_forward_0_0/pallas_call | solution.py:406
  158.8 12.2 %attn_forward_1_1.1 = (f32[768,768]{1,0:T(8,128)}, bf16[768,768]{1,0:T(8,128)(2,1)}) custom-call(s32[4]{0:T(128)S(1)} %pad_add_fusion.1.meta, f32[768,768]{1,0:T(8,128)} %get-tuple-element.90.refs_0_, bf16[768,768]{1,0:T(8,128)(2,1)} %get-tuple-element.91.refs_1_, bf16[768,768]{1,0:T(8,128)(2,1)} %copy-done.99, ...), custom_call_target="tpu_custom_call" | custom-call | flops 2264924160 | bytes 10652176 | tf_op jit(solution)/shard_map/attn_forward_1_1/pallas_call | solution.py:406
  176.4 13.3 %attn_forward_0_1.1 = (f32[768,768]{1,0:T(8,128)}, bf16[768,768]{1,0:T(8,128)(2,1)}, bf16[768,768]{1,0:T(8,128)(2,1)}, bf16[2,768,576]{2,1,0:T(8,128)(2,1)}, bf1...) custom-call(s32[4]{0:T(128)S(1)} %pad_add_fusion.meta, ...), custom_call_target="tpu_custom_call" | custom-call | flops 2264924160 | bytes 18912784 | tf_op jit(solution)/shard_map/attn_forward_0_1/pallas_call | solution.py:406
  193.7 6.3 collective-permute-done.66.refs_11_
  222.1 9.4 %ffn_forward_1_1.1 = (f32[768,768]{1,0:T(8,128)}, bf16[768,768]{1,0:T(8,128)(2,1)}) custom-call(s32[4]{0:T(128)S(1)} %pad_add_fusion.1.meta, f32[768,768]{1,0:T(8,128)} %get-tuple-element.92.refs_0_, bf16[768,768]{1,0:T(8,128)(2,1)} %get-tuple-element.93.refs_1_, bf16[768,768]{1,0:T(8,128)(2,1)} %copy-done.94, bf16[768,768]{1,0:T(8,128)(2,1)} %get-tuple-element.194.refs_3_, ...), custom_call_target="tpu_custom_call" | custom-call | flops 3623878656 | bytes 13000720 | tf_op jit(solution)/shard_map/ffn_forward_1_1/pallas_call | solution.py:406
  236.2 11.2 %ffn_forward_0_1.1 = (f32[768,768]{1,0:T(8,128)}, bf16[768,768]{1,0:T(8,128)(2,1)}, f32[768,768]{1,0:T(8,128)}, f32[768,1]{1,0:T(8,128)}, bf16[768,768]{1,0:T(8,...) custom-call(s32[4]{0:T(128)S(1)} %pad_add_fusion.meta, f32[768,768]{1,0:T(8,128)} %get-tuple-element.83.refs_0_, ...), custom_call_target="tpu_custom_call" | custom-call | flops 3623878656 | bytes 21261328 | tf_op jit(solution)/shard_map/ffn_forward_0_1/pallas_call | solution.py:406
  257.5 19.9 %contrast.1 = (f32[16,128]{1,0:T(8,128)S(1)}, f32[3,768]{1,0:T(4,128)S(1)}) custom-call(s32[1]{0:T(128)S(6)} %copy.98.count, f32[3,1]{1,0:T(4,128)S(1)} %copy.63.inv_q, f32[3,1]{1,0:T(4,128)S(1)} %copy.64.inv_k, f32[3,768]{1,0:T(4,128)S(1)} %bitcast.256, f32[3,768]{1,0:T(4,128)S(1)} %bitcast.255), custom_call_target="tpu_custom_call" | custom-call | tf_op jit(solution)/shard_map/contrast/pallas_call | solution.py:603
  277.5 10.4 %ffn_backward_1.1 = (f32[768,768]{1,0:T(8,128)}, bf16[768,768]{1,0:T(8,128)(2,1)}, bf16[768,768]{1,0:T(8,128)(2,1)}, bf16[2,768,768]{2,1,0:T(8,128)(2,1)}, f32[8,768]{1,0:T(8,128)S(1)}, /*index=5*/f32[8,768]{1,0:T(8,128)S(1)}) custom-call(s32[4]{0:T(128)S(1)} %pad_add_fusion.meta, f32[3,1,768]{2,1,0:T(1,128)S(1)} %reshape.164.refs_0_, ...), custom_call_target="tpu_custom_call" | custom-call | flops 3623878656 | bytes 16582672 | tf_op jit(solution)/shard_map/ffn_backward_1/pallas_call | solution.py:406
  291.7 7.8 %ffn_weights_1.1 = (f32[2,768,768]{2,1,0:T(8,128)}, f32[2,768,768]{2,1,0:T(8,128)}) custom-call(bf16[768,768]{1,0:T(8,128)(2,1)S(1)} %copy-done.54, bf16[2,768,768]{2,1,0:T(8,128)(2,1)} %get-tuple-element.134.active, bf16[768,768]{1,0:T(8,128)(2,1)} %get-tuple-element.135.normed, bf16[2,768,768]{2,1,0:T(8,128)(2,1)} %get-tuple-element.136.inner), custom_call_target="tpu_custom_call" | custom-call | flops 3623878656 | bytes 16515072 | tf_op jit(solution)/shard_map/ffn_weights_1/pallas_call | solution.py:406
  307.9 16.8 %attn_backward_1.1 = (f32[768,768]{1,0:T(8,128)}, bf16[768,768]{1,0:T(8,128)(2,1)}, bf16[768,768]{1,0:T(8,128)(2,1)}, bf16[2,768,576]{2,1,0:T(8,128)(2,1)}, f32[8,768]{1,0:T(8,128)S(1)}, /*index=5*/f32[8,576]{1,0:T(8,128)S(1)}) custom-call(s32[4]{0:T(128)S(1)} %pad_add_fusion.meta, f32[768,768]{1,0:T(8,128)} %get-tuple-element.101.refs_0_, ...), custom_call_target="tpu_custom_call" | custom-call | flops 3170893824 | bytes 18926608 | tf_op jit(solution)/shard_map/attn_backward_1/pallas_call | solution.py:406
  326.6 6.0 attn_weights_1.1
  336.4 11.3 %ffn_backward_0.1 = (f32[768,768]{1,0:T(8,128)}, bf16[768,768]{1,0:T(8,128)(2,1)}, bf16[768,768]{1,0:T(8,128)(2,1)}, bf16[2,768,768]{2,1,0:T(8,128)(2,1)}, f32[8,768]{1,0:T(8,128)S(1)}, /*index=5*/f32[8,768]{1,0:T(8,128)S(1)}) custom-call(s32[4]{0:T(128)S(1)} %pad_add_fusion.meta, f32[768,768]{1,0:T(8,128)} %get-tuple-element.107.refs_0_, ...), custom_call_target="tpu_custom_call" | custom-call | flops 3623878656 | bytes 20112400 | tf_op jit(solution)/shard_map/ffn_backward_0/pallas_call | solution.py:406
  349.1 7.8 %ffn_weights_0.1 = (f32[2,768,768]{2,1,0:T(8,128)}, f32[2,768,768]{2,1,0:T(8,128)}) custom-call(bf16[768,768]{1,0:T(8,128)(2,1)S(1)} %copy-done.52, bf16[2,768,768]{2,1,0:T(8,128)(2,1)} %get-tuple-element.129.active, bf16[768,768]{1,0:T(8,128)(2,1)} %get-tuple-element.130.normed, bf16[2,768,768]{2,1,0:T(8,128)(2,1)} %get-tuple-element.131.inner), custom_call_target="tpu_custom_call" | custom-call | flops 3623878656 | bytes 16515072 | tf_op jit(solution)/shard_map/ffn_weights_0/pallas_call | solution.py:406
  364.8 4.9 fusion.24
  375.5 16.9 %attn_backward_0.1 = (f32[768,768]{1,0:T(8,128)}, bf16[768,768]{1,0:T(8,128)(2,1)}, bf16[768,768]{1,0:T(8,128)(2,1)}, bf16[2,768,576]{2,1,0:T(8,128)(2,1)}, f32[8,768]{1,0:T(8,128)S(1)}, /*index=5*/f32[8,576]{1,0:T(8,128)S(1)}) custom-call(s32[4]{0:T(128)S(1)} %pad_add_fusion.meta, f32[768,768]{1,0:T(8,128)} %get-tuple-element.112.refs_0_, ...), custom_call_target="tpu_custom_call" | custom-call | flops 3170893824 | bytes 18926608 | tf_op jit(solution)/shard_map/attn_backward_0/pallas_call | solution.py:406
  392.9 63.2 %total_over.1 = f32[24,768]{1,0:T(8,128)S(1)} custom-call(f32[24,768]{1,0:T(8,128)S(1)} %concatenate.87.v_ref), custom_call_target="tpu_custom_call" | custom-call | tf_op jit(solution)/shard_map/total_over/pallas_call | solution.py:755
  464.5 6.4 attn_weights_0.1
  478.4 9.5 %collective-permute-done.89 = f32[2,96,768]{2,1,0:T(8,128)} collective-permute-done((f32[2,96,768]{2,1,0:T(8,128)S(1)}, f32[2,96,768]{2,1,0:T(8,128)}, u32[]{:S(2)}, u32[]{:S(2)}) %collective-permute-start.89) | collective-permute-done | bytes 589856 | tf_op jit(solution)/shard_map/ppermute | solution.py:447
  492.1 53.2 %collective-permute-done.98 = f32[96,768]{1,0:T(8,128)S(1)} collective-permute-done((f32[96,768]{1,0:T(8,128)S(1)}, f32[96,768]{1,0:T(8,128)S(1)}, u32[]{:S(2)}, u32[]{:S(2)}) %collective-permute-start.98) | collective-permute-done | bytes 294944 | tf_op jit(solution)/shard_map/ppermute | solution.py:447
  553.1 7.5 %collective-permute-done.90 = f32[96,768]{1,0:T(8,128)S(1)} collective-permute-done((f32[96,768]{1,0:T(8,128)S(1)}, f32[96,768]{1,0:T(8,128)S(1)}, u32[]{:S(2)}, u32[]{:S(2)}) %collective-permute-start.90) | collective-permute-done | bytes 294944 | tf_op jit(solution)/shard_map/ppermute | solution.py:447
  571.4 6.0 collective-permute-done.92
  579.0 7.5 %collective-permute-done.82 = f32[96,768]{0,1:T(8,128)} collective-permute-done((f32[96,768]{0,1:T(8,128)}, f32[96,768]{0,1:T(8,128)}, u32[]{:S(2)}, u32[]{:S(2)}) %collective-permute-start.82) | collective-permute-done | bytes 294944 | tf_op jit(solution)/shard_map/ppermute | solution.py:447
  591.8 5.1 collective-permute-done.93
  597.1 5.5 collective-permute-done.76
  604.2 9.1 %collective-permute-done.85 = f32[2,96,768]{2,1,0:T(8,128)S(1)} collective-permute-done((f32[2,96,768]{2,1,0:T(8,128)S(1)}, f32[2,96,768]{2,1,0:T(8,128)S(1)}, u32[]{:S(2)}, u32[]{:S(2)}) %collective-permute-start.85) | collective-permute-done | bytes 589856 | tf_op jit(solution)/shard_map/ppermute | solution.py:447
  617.0 21.1 %collective-permute-done.86 = f32[96,768]{1,0:T(8,128)} collective-permute-done((f32[96,768]{1,0:T(8,128)}, f32[96,768]{1,0:T(8,128)}, u32[]{:S(2)}, u32[]{:S(2)}) %collective-permute-start.86) | collective-permute-done | bytes 294944 | tf_op jit(solution)/shard_map/ppermute | solution.py:447
  640.9 5.5 collective-permute-done.78
  (597 shorter events, 235.5 us)
Async XLA Ops:
  3.6 27.9 %collective-permute-start.6 = (f32[2,2304]{1,0:T(2,128)S(1)}, f32[2,2304]{1,0:T(2,128)S(1)}, u32[]{:S(2)}, u32[]{:S(2)}) collective-permute-start(f32[2,2304]{1,0:T(2,128)S(1)} %pad_maximum_fusion.6), channel_id=1, source_target_pairs={{0,2},{1,3},{2,0},{3,1},{4,6},{5,7},{6,4},{7,5},{8,10},{9,11},{10,... | collective-permute-start | bytes 55304 | tf_op jit(solution)/shard_map/ppermute | solution.py:441
  6.7 26.1 %collective-permute-start.37 = (bf16[192,768]{1,0:T(8,128)(2,1)}, bf16[192,768]{1,0:T(8,128)(2,1)S(1)}, u32[]{:S(2)}, u32[]{:S(2)}) collective-permute-start(bf16[192,768]{1,0:T(8,128)(2,1)} %fusion.8), channel_id=1, source_target_pairs={{0,2},{1,3},{2,0},{3,1},{4,6},{5,7},{6,4},{7,5},{8,10},{9,11},{10,... | collective-permute-start | bytes 884744 | tf_op jit(solution)/shard_map/ppermute | solution.py:441
  12.4 20.7 %collective-permute-start.43 = (bf16[192,768]{1,0:T(8,128)(2,1)}, bf16[192,768]{1,0:T(8,128)(2,1)S(1)}, u32[]{:S(2)}, u32[]{:S(2)}) collective-permute-start(bf16[192,768]{1,0:T(8,128)(2,1)} %dynamic-slice_bitcast_fusion.19), channel_id=1, source_target_pairs={{0,2},{1,3},{2,0},{3,1},{4,6},{5,7},{6,4},{7,5},{8,10},{9,11},{10,... | collective-permute-start | bytes 884744 | tf_op jit(solution)/shard_map/ppermute | solution.py:441
  15.3 20.4 %collective-permute-start.48 = (bf16[192,768]{1,0:T(8,128)(2,1)}, bf16[192,768]{1,0:T(8,128)(2,1)}, u32[]{:S(2)}, u32[]{:S(2)}) collective-permute-start(bf16[192,768]{1,0:T(8,128)(2,1)} %dynamic-slice_bitcast_fusion.18), channel_id=1, source_target_pairs={{0,2},{1,3},{2,0},{3,1},{4,6},{5,7},{6,4},{7,5},{8,10},{9,11},{10,... | collective-permute-start | bytes 884744 | tf_op jit(solution)/shard_map/ppermute | solution.py:441
  33.1 19.9 %collective-permute-start.36 = (bf16[384,768]{1,0:T(8,128)(2,1)}, bf16[384,768]{1,0:T(8,128)(2,1)S(1)}, u32[]{:S(2)}, u32[]{:S(2)}) collective-permute-start(bf16[384,768]{1,0:T(8,128)(2,1)} %param.22), channel_id=1, source_target_pairs={{0,1},{1,0},{2,3},{3,2},{4,5},{5,4},{6,7},{7,6},{8,9},{9,8},{10,11... | collective-permute-start | bytes 1769480 | tf_op jit(solution)/shard_map/ppermute | solution.py:444
  47.3 26.6 %collective-permute-start = (bf16[384,768]{1,0:T(8,128)(2,1)}, bf16[384,768]{1,0:T(8,128)(2,1)S(1)}, u32[]{:S(2)}, u32[]{:S(2)}) collective-permute-start(bf16[384,768]{1,0:T(8,128)(2,1)} %param.21), channel_id=1, source_target_pairs={{0,1},{1,0},{2,3},{3,2},{4,5},{5,4},{6,7},{7,6},{8,9},{9,8},{10,11... | collective-permute-start | bytes 1769480 | tf_op jit(solution)/shard_map/ppermute | solution.py:444
  74.0 35.4 %collective-permute-start.42 = (bf16[768,768]{1,0:T(8,128)(2,1)}, bf16[768,768]{1,0:T(8,128)(2,1)S(1)}, u32[]{:S(2)}, u32[]{:S(2)}) collective-permute-start(bf16[768,768]{1,0:T(8,128)(2,1)} %get-tuple-element.89.refs_1_), channel_id=1, source_target_pairs={{0,1},{1,0},{2,3},{3,2},{4,5},{5,4},{6,7},{7,6},{8,9},{9,8},{10,11... | collective-permute-start | bytes 3538952 | tf_op jit(solution)/shard_map/ppermute | solution.py:444
  91.0 36.6 %collective-permute-start.7 = (bf16[768,768]{1,0:T(8,128)(2,1)}, bf16[768,768]{1,0:T(8,128)(2,1)S(1)}, u32[]{:S(2)}, u32[]{:S(2)}) collective-permute-start(bf16[768,768]{1,0:T(8,128)(2,1)} %get-tuple-element.80.refs_1_), channel_id=1, source_target_pairs={{0,1},{1,0},{2,3},{3,2},{4,5},{5,4},{6,7},{7,6},{8,9},{9,8},{10,11... | collective-permute-start | bytes 3538952 | tf_op jit(solution)/shard_map/ppermute | solution.py:444
  120.0 37.8 %collective-permute-start.53 = (bf16[768,768]{1,0:T(8,128)(2,1)}, bf16[768,768]{1,0:T(8,128)(2,1)S(1)}, u32[]{:S(2)}, u32[]{:S(2)}) collective-permute-start(bf16[768,768]{1,0:T(8,128)(2,1)} %get-tuple-element.91.refs_1_), channel_id=1, source_target_pairs={{0,1},{1,0},{2,3},{3,2},{4,5},{5,4},{6,7},{7,6},{8,9},{9,8},{10,11... | collective-permute-start | bytes 3538952 | tf_op jit(solution)/shard_map/ppermute | solution.py:444
  139.8 35.6 %collective-permute-start.18 = (bf16[768,768]{1,0:T(8,128)(2,1)}, bf16[768,768]{1,0:T(8,128)(2,1)S(1)}, u32[]{:S(2)}, u32[]{:S(2)}) collective-permute-start(bf16[768,768]{1,0:T(8,128)(2,1)} %get-tuple-element.82.refs_1_), channel_id=1, source_target_pairs={{0,1},{1,0},{2,3},{3,2},{4,5},{5,4},{6,7},{7,6},{8,9},{9,8},{10,11... | collective-permute-start | bytes 3538952 | tf_op jit(solution)/shard_map/ppermute | solution.py:444
  171.0 50.1 %collective-permute-start.59 = (bf16[768,768]{1,0:T(8,128)(2,1)}, bf16[768,768]{1,0:T(8,128)(2,1)S(1)}, u32[]{:S(2)}, u32[]{:S(2)}) collective-permute-start(bf16[768,768]{1,0:T(8,128)(2,1)} %get-tuple-element.93.refs_1_), channel_id=1, source_target_pairs={{0,1},{1,0},{2,3},{3,2},{4,5},{5,4},{6,7},{7,6},{8,9},{9,8},{10,11... | collective-permute-start | bytes 3538952 | tf_op jit(solution)/shard_map/ppermute | solution.py:444
  190.5 44.6 %collective-permute-start.24 = (bf16[768,768]{1,0:T(8,128)(2,1)}, bf16[768,768]{1,0:T(8,128)(2,1)S(1)}, u32[]{:S(2)}, u32[]{:S(2)}) collective-permute-start(bf16[768,768]{1,0:T(8,128)(2,1)} %get-tuple-element.84.refs_1_), channel_id=1, source_target_pairs={{0,1},{1,0},{2,3},{3,2},{4,5},{5,4},{6,7},{7,6},{8,9},{9,8},{10,11... | collective-permute-start | bytes 3538952 | tf_op jit(solution)/shard_map/ppermute | solution.py:444
  287.9 20.0 %collective-permute-start.71 = (bf16[768,768]{1,0:T(8,128)(2,1)}, bf16[768,768]{1,0:T(8,128)(2,1)}, u32[]{:S(2)}, u32[]{:S(2)}) collective-permute-start(bf16[768,768]{1,0:T(8,128)(2,1)} %get-tuple-element.102), channel_id=1, source_target_pairs={{0,1},{1,0},{2,3},{3,2},{4,5},{5,4},{6,7},{7,6},{8,9},{9,8},{10,11... | collective-permute-start | bytes 3538952 | tf_op jit(solution)/shard_map/ppermute | solution.py:444
  302.8 57.5 %collective-permute-start.95 = (f32[2,2,2,96,768]{4,3,2,1,0:T(8,128)}, f32[2,2,2,96,768]{4,3,2,1,0:T(8,128)}, u32[]{:S(2)}, u32[]{:S(2)}) collective-permute-start(f32[2,2,2,96,768]{4,3,2,1,0:T(8,128)} %dynamic-slice_bitcast_fusion), channel_id=1, source_target_pairs={{0,4},{4,0},{8,12},{12,8},{16,20},{20,16},{24,28},{28,24},{1,5},{5... | collective-permute-start | bytes 7077896 | tf_op jit(solution)/shard_map/ppermute | solution.py:447
  306.5 63.2 %collective-permute-start.87 = (f32[2,2,2,96,768]{4,3,2,1,0:T(8,128)}, f32[2,2,2,96,768]{4,3,2,1,0:T(8,128)}, u32[]{:S(2)}, u32[]{:S(2)}) collective-permute-start(f32[2,2,2,96,768]{4,3,2,1,0:T(8,128)} %bitcast.91), channel_id=1, source_target_pairs={{0,2},{1,3},{2,0},{3,1},{4,6},{5,7},{6,4},{7,5},{8,10},{9,11},{10,... | collective-permute-start | bytes 7077896 | tf_op jit(solution)/shard_map/ppermute | solution.py:441
  336.3 138.5 %collective-permute-start.79 = (f32[2,2,2,96,768]{4,3,2,1,0:T(8,128)}, f32[2,2,2,96,768]{4,3,2,1,0:T(8,128)}, u32[]{:S(2)}, u32[]{:S(2)}) collective-permute-start(f32[2,2,2,96,768]{4,3,2,1,0:T(8,128)} %dynamic-slice_bitcast_fusion.2), channel_id=1, source_target_pairs={{0,8},{4,12},{8,0},{12,4},{16,24},{20,28},{24,16},{28,20},{1,9},{5... | collective-permute-start | bytes 7077896 | tf_op jit(solution)/shard_map/ppermute | solution.py:447
  347.7 26.4 %collective-permute-start.73 = (bf16[768,768]{1,0:T(8,128)(2,1)}, bf16[768,768]{1,0:T(8,128)(2,1)S(1)}, u32[]{:S(2)}, u32[]{:S(2)}) collective-permute-start(bf16[768,768]{1,0:T(8,128)(2,1)} %get-tuple-element.113), channel_id=1, source_target_pairs={{0,1},{1,0},{2,3},{3,2},{4,5},{5,4},{6,7},{7,6},{8,9},{9,8},{10,11... | collective-permute-start | bytes 3538952 | tf_op jit(solution)/shard_map/ppermute | solution.py:444
  360.1 188.8 %collective-permute-start.91 = (f32[2,2,2,96,768]{4,3,2,1,0:T(8,128)}, f32[2,2,2,96,768]{4,3,2,1,0:T(8,128)}, u32[]{:S(2)}, u32[]{:S(2)}) collective-permute-start(f32[2,2,2,96,768]{4,3,2,1,0:T(8,128)} %dynamic-slice_bitcast_fusion.1), channel_id=1, source_target_pairs={{0,4},{4,0},{8,12},{12,8},{16,20},{20,16},{24,28},{28,24},{1,5},{5... | collective-permute-start | bytes 7077896 | tf_op jit(solution)/shard_map/ppermute | solution.py:447
  363.5 93.9 %collective-permute-start.96 = (f32[2,2,96,768]{3,2,1,0:T(8,128)}, f32[2,2,96,768]{3,2,1,0:T(8,128)}, u32[]{:S(2)}, u32[]{:S(2)}) collective-permute-start(f32[2,2,96,768]{3,2,1,0:T(8,128)} %slice_bitcast_fusion), channel_id=1, source_target_pairs={{0,2},{1,3},{2,0},{3,1},{4,6},{5,7},{6,4},{7,5},{8,10},{9,11},{10,... | collective-permute-start | bytes 3538952 | tf_op jit(solution)/shard_map/ppermute | solution.py:441
  369.7 191.0 %collective-permute-start.83 = (f32[2,2,2,96,768]{4,3,2,1,0:T(8,128)}, f32[2,2,2,96,768]{4,3,2,1,0:T(8,128)}, u32[]{:S(2)}, u32[]{:S(2)}) collective-permute-start(f32[2,2,2,96,768]{4,3,2,1,0:T(8,128)} %bitcast.82), channel_id=1, source_target_pairs={{0,2},{1,3},{2,0},{3,1},{4,6},{5,7},{6,4},{7,5},{8,10},{9,11},{10,... | collective-permute-start | bytes 7077896 | tf_op jit(solution)/shard_map/ppermute | solution.py:441
  374.1 87.5 %collective-permute-start.88 = (f32[2,2,96,768]{3,2,1,0:T(8,128)}, f32[2,2,96,768]{3,2,1,0:T(8,128)}, u32[]{:S(2)}, u32[]{:S(2)}) collective-permute-start(f32[2,2,96,768]{3,2,1,0:T(8,128)} %dynamic-slice_bitcast_fusion.4), channel_id=1, source_target_pairs={{0,4},{4,0},{8,12},{12,8},{16,20},{20,16},{24,28},{28,24},{1,5},{5... | collective-permute-start | bytes 3538952 | tf_op jit(solution)/shard_map/ppermute | solution.py:447
  463.3 24.7 %collective-permute-start.89 = (f32[2,96,768]{2,1,0:T(8,128)S(1)}, f32[2,96,768]{2,1,0:T(8,128)}, u32[]{:S(2)}, u32[]{:S(2)}) collective-permute-start(f32[2,96,768]{2,1,0:T(8,128)S(1)} %dynamic-slice_bitcast_fusion.8), channel_id=1, source_target_pairs={{0,8},{4,12},{8,0},{12,4},{16,24},{20,28},{24,16},{28,20},{1,9},{5... | collective-permute-start | bytes 1769480 | tf_op jit(solution)/shard_map/ppermute | solution.py:447
  477.3 71.1 %collective-permute-start.80 = (f32[2,2,96,768]{3,2,1,0:T(8,128)S(1)}, f32[2,2,96,768]{3,2,1,0:T(8,128)S(1)}, u32[]{:S(2)}, u32[]{:S(2)}) collective-permute-start(f32[2,2,96,768]{3,2,1,0:T(8,128)S(1)} %slice_bitcast_fusion.4), channel_id=1, source_target_pairs={{0,2},{1,3},{2,0},{3,1},{4,6},{5,7},{6,4},{7,5},{8,10},{9,11},{10,... | collective-permute-start | bytes 3538952 | tf_op jit(solution)/shard_map/ppermute | solution.py:441
  487.9 79.4 %collective-permute-start.75 = (f32[2,2,2,96,768]{4,3,2,1,0:T(8,128)}, f32[2,2,2,96,768]{4,3,2,1,0:T(8,128)}, u32[]{:S(2)}, u32[]{:S(2)}) collective-permute-start(f32[2,2,2,96,768]{4,3,2,1,0:T(8,128)} %dynamic-slice_bitcast_fusion.3), channel_id=1, source_target_pairs={{0,8},{4,12},{8,0},{12,4},{16,24},{20,28},{24,16},{28,20},{1,9},{5... | collective-permute-start | bytes 7077896 | tf_op jit(solution)/shard_map/ppermute | solution.py:447
  490.3 55.0 %collective-permute-start.98 = (f32[96,768]{1,0:T(8,128)S(1)}, f32[96,768]{1,0:T(8,128)S(1)}, u32[]{:S(2)}, u32[]{:S(2)}) collective-permute-start(f32[96,768]{1,0:T(8,128)S(1)} %dynamic-slice_bitcast_fusion.12), channel_id=1, source_target_pairs={{0,16},{4,20},{8,24},{12,28},{16,0},{20,4},{24,8},{28,12},{1,17},{... | collective-permute-start | bytes 884744 | tf_op jit(solution)/shard_map/ppermute | solution.py:447
  552.1 25.3 %collective-permute-start.92 = (f32[2,2,96,768]{3,2,1,0:T(8,128)}, f32[2,2,96,768]{3,2,1,0:T(8,128)}, u32[]{:S(2)}, u32[]{:S(2)}) collective-permute-start(f32[2,2,96,768]{3,2,1,0:T(8,128)} %slice_bitcast_fusion.2), channel_id=1, source_target_pairs={{0,2},{1,3},{2,0},{3,1},{4,6},{5,7},{6,4},{7,5},{8,10},{9,11},{10,... | collective-permute-start | bytes 3538952 | tf_op jit(solution)/shard_map/ppermute | solution.py:441
  564.5 25.7 %collective-permute-start.84 = (f32[2,2,96,768]{3,2,1,0:T(8,128)}, f32[2,2,96,768]{3,2,1,0:T(8,128)}, u32[]{:S(2)}, u32[]{:S(2)}) collective-permute-start(f32[2,2,96,768]{3,2,1,0:T(8,128)} %dynamic-slice_bitcast_fusion.5), channel_id=1, source_target_pairs={{0,4},{4,0},{8,12},{12,8},{16,20},{20,16},{24,28},{28,24},{1,5},{5... | collective-permute-start | bytes 3538952 | tf_op jit(solution)/shard_map/ppermute | solution.py:447
  566.3 20.2 %collective-permute-start.82 = (f32[96,768]{0,1:T(8,128)}, f32[96,768]{0,1:T(8,128)}, u32[]{:S(2)}, u32[]{:S(2)}) collective-permute-start(f32[96,768]{0,1:T(8,128)} %bitcast.282), channel_id=1, source_target_pairs={{0,16},{4,20},{8,24},{12,28},{16,0},{20,4},{24,8},{28,12},{1,17},{... | collective-permute-start | bytes 884744 | tf_op jit(solution)/shard_map/ppermute | solution.py:447
  570.2 32.4 %collective-permute-start.76 = (f32[2,2,96,768]{3,2,1,0:T(8,128)S(1)}, f32[2,2,96,768]{3,2,1,0:T(8,128)S(1)}, u32[]{:S(2)}, u32[]{:S(2)}) collective-permute-start(f32[2,2,96,768]{3,2,1,0:T(8,128)S(1)} %slice_bitcast_fusion.6), channel_id=1, source_target_pairs={{0,2},{1,3},{2,0},{3,1},{4,6},{5,7},{6,4},{7,5},{8,10},{9,11},{10,... | collective-permute-start | bytes 3538952 | tf_op jit(solution)/shard_map/ppermute | solution.py:441
  591.7 21.6 %collective-permute-start.85 = (f32[2,96,768]{2,1,0:T(8,128)S(1)}, f32[2,96,768]{2,1,0:T(8,128)S(1)}, u32[]{:S(2)}, u32[]{:S(2)}) collective-permute-start(f32[2,96,768]{2,1,0:T(8,128)S(1)} %dynamic-slice_bitcast_fusion.9), channel_id=1, source_target_pairs={{0,8},{4,12},{8,0},{12,4},{16,24},{20,28},{24,16},{28,20},{1,9},{5... | collective-permute-start | bytes 1769480 | tf_op jit(solution)/shard_map/ppermute | solution.py:447
  614.2 23.9 %collective-permute-start.86 = (f32[96,768]{1,0:T(8,128)}, f32[96,768]{1,0:T(8,128)}, u32[]{:S(2)}, u32[]{:S(2)}) collective-permute-start(f32[96,768]{1,0:T(8,128)} %dynamic-slice_bitcast_fusion.15), channel_id=1, source_target_pairs={{0,16},{4,20},{8,24},{12,28},{16,0},{20,4},{24,8},{28,12},{1,17},{... | collective-permute-start | bytes 884744 | tf_op jit(solution)/shard_map/ppermute | solution.py:447
  614.7 31.7 %collective-permute-start.78 = (f32[96,768]{0,1:T(8,128)S(1)}, f32[96,768]{0,1:T(8,128)S(1)}, u32[]{:S(2)}, u32[]{:S(2)}) collective-permute-start(f32[96,768]{0,1:T(8,128)S(1)} %bitcast.283), channel_id=1, source_target_pairs={{0,16},{4,20},{8,24},{12,28},{16,0},{20,4},{24,8},{28,12},{1,17},{... | collective-permute-start | bytes 884744 | tf_op jit(solution)/shard_map/ppermute | solution.py:447
  (173 other events, 2318.5 us)

commit v2 on v1

v2 whole, which is shorter than its diff:
```python
import functools
import math

import jax
import jax.numpy as jnp
from jax import lax
from jax.experimental import pallas as pl
from jax.experimental.pallas import tpu as pltpu
from jax.sharding import PartitionSpec as P

D = 768
HEAD = 64
SEQ = 256
LAYERS = 2
BLOB = 768
EPS = 1e-06
TEMPER = 0.05
FILL = -1e30
BF = jnp.bfloat16
F32 = jnp.float32
MESH = pl.DeviceIdType.MESH
SCALE = HEAD ** (-0.5)
MIB = 2**20


def mm(a, b):
    return jnp.dot(a, b, preferred_element_type=F32)


def mm_nt(a, b):
    return lax.dot_general(a, b, (((1,), (1,)), ((), ())), preferred_element_type=F32)


def mm_tn(a, b):
    return lax.dot_general(a, b, (((0,), (0,)), ((), ())), preferred_element_type=F32)


def norm(v, gain, shift):
    center = v - jnp.mean(v, axis=-1, keepdims=True)
    rate = lax.rsqrt(jnp.mean(center * center, axis=-1, keepdims=True) + EPS)
    xhat = center * rate
    return xhat, rate, xhat * gain + shift


def norm_back(g, xhat, rate, gain):
    gx = g * gain
    return rate * (
        gx
        - jnp.mean(gx, axis=-1, keepdims=True)
        - xhat * jnp.mean(gx * xhat, axis=-1, keepdims=True)
    )


def rows(v):
    return jnp.sum(v, axis=0, keepdims=True)


def groups():
    return [(layer, e, kind) for layer in range(LAYERS) for kind in range(2) for e in range(2)]


def forward(dp_size, nc, *refs):
    refs = list(refs)

    def take(n):
        return [refs.pop(0) for _ in range(n)]

    meta, count = take(2)
    x_in, blob_a, w_in, w_down, gains, shifts = [take(2) for _ in range(6)]
    bias, inv_q, inv_k = take(3)
    saves = dict(
        zip(("hidden", "proj", "probs", "mixed", "v1", "normed", "active", "slope", "v2"), take(9))
    )
    far_out, pair_out, grad_out = take(3)
    low, base, acc, send, recv, own_a, own_f, far = take(8)
    v_st, proj_st, probs_st, mixed_st, active_st, slope_st = take(6)
    far_bias, sums, held = take(3)
    y_send, y_recv, p_send, p_recv, x_send, x_recv, own_sem, save_sem, c_send, c_recv, b_sem = take(11)

    d = lax.axis_index("dp")
    t = lax.axis_index("tensor")
    core = t & 1
    half = t // 2
    q = d & 3
    share = x_in[0].shape[0]
    far_id, core_id, x_id, z_id = (d, t ^ 2), (d, t ^ 1), (d ^ 1, t), (d ^ 2, t)
    dp_bits = dp_size.bit_length() - 1
    bit_ids = [(d ^ (1 << k), t) for k in reversed(range(dp_bits))] + [far_id]
    greet(bit_ids + [core_id])

    def remote(src, dst, sems, at, device):
        return pltpu.make_async_remote_copy(
            src_ref=src,
            dst_ref=dst,
            send_sem=sems[0].at[at],
            recv_sem=sems[1].at[at],
            device_id=device,
            device_id_type=MESH,
        )

    mine = pl.ds(pl.multiple_of(core * share, 16), share)
    x_local = []
    x_remote = []
    for e in range(2):
        x_local.append(pltpu.make_async_copy(x_in[e], low.at[e, mine], own_sem.at[e, 2]))
        x_remote.append(remote(x_in[e], low.at[e, mine], (x_send, x_recv), e, core_id))

    def load_a(e, layer):
        return [pltpu.make_async_copy(blob_a[e].at[layer], own_a.at[e], own_sem.at[e, 0])]

    def load_f(e, layer):
        return [
            pltpu.make_async_copy(w_in[e].at[layer], own_f.at[e, 0], own_sem.at[e, 1]),
            pltpu.make_async_copy(w_down[e].at[layer], own_f.at[e, 1], own_sem.at[e, 3]),
        ]

    x_local[0].start()
    x_remote[0].start()
    for copy in load_a(0, 0):
        copy.start()
    b_copy = pltpu.make_async_remote_copy(
        src_ref=bias,
        dst_ref=far_bias,
        send_sem=b_sem.at[0],
        recv_sem=b_sem.at[1],
        device_id=far_id,
        device_id_type=MESH,
    )
    b_copy.start()
    x_local[1].start()
    x_remote[1].start()
    for copy in load_a(1, 0) + load_f(0, 0) + load_f(1, 0):
        copy.start()

    n = BLOB // 4
    third = n // 3
    order = groups()
    moves = []
    for g, (layer, e, kind) in enumerate(order):
        u = layer * 2 + e

        def at(quarter, start, size, which=None):
            row = pl.ds(pl.multiple_of(quarter * n + start, 16), size)
            if kind == 0:
                return far.at[u, 0, row]
            return far.at[u, pl.ds(1, 2), row] if which is None else far.at[u, 1 + which, row]

        def source(which, quarter, start, size):
            row = pl.ds(pl.multiple_of(quarter * n + start, 16), size)
            ref = blob_a[e] if kind == 0 else (w_in[e], w_down[e])[which]
            return ref.at[layer, row]

        sems = (y_send, y_recv)
        made = {}
        for w in range(1 + kind):
            made["y", w] = remote(source(w, q, 0, n), at(q, 0, n, w), sems, (g, w), far_id)
            made["t", w] = remote(
                source(w, q ^ 3, 0, third), at(q ^ 3, 0, third, w), sems, (g, 2 + w), far_id
            )
        made["x2"] = remote(at(q, 0, n), at(q, 0, n), sems, (g, 4), x_id)
        made["z2"] = remote(at(q, 0, n), at(q, 0, n), sems, (g, 5), z_id)
        made["x3"] = remote(at(q ^ 2, third, third), at(q ^ 2, third, third), sems, (g, 6), x_id)
        made["z3"] = remote(at(q ^ 1, 2 * third, third), at(q ^ 1, 2 * third, third), sems, (g, 7), z_id)
        got = dict(made)
        got["x2"] = remote(at(q ^ 1, 0, n), at(q ^ 1, 0, n), sems, (g, 4), x_id)
        got["z2"] = remote(at(q ^ 2, 0, n), at(q ^ 2, 0, n), sems, (g, 5), z_id)
        got["x3"] = remote(at(q ^ 3, third, third), at(q ^ 3, third, third), sems, (g, 6), x_id)
        got["z3"] = remote(at(q ^ 3, 2 * third, third), at(q ^ 3, 2 * third, third), sems, (g, 7), z_id)
        moves.append((made, got, kind))

    def start_y(g, name):
        made, _, kind = moves[g]
        for w in range(1 + kind):
            made[name, w].start()

    start_y(0, "y")
    for g in range(1, len(order)):
        start_y(g, "y")
        start_y(g - 1, "t")
    start_y(len(order) - 1, "t")

    def pass_first(g):
        made, got, kind = moves[g]
        for w in range(1 + kind):
            got["y", w].wait_recv()
        made["x2"].start()
        made["z2"].start()

    def pass_second(g):
        made, got, _ = moves[g]
        got["x2"].wait_recv()
        got["z2"].wait_recv()
        made["x3"].start()
        made["z3"].start()

    def ready(g):
        _, got, kind = moves[g]
        got["x3"].wait_recv()
        got["z3"].wait_recv()
        for w in range(1 + kind):
            got["t", w].wait_recv()

    def save(name, layer, src, k):
        return pltpu.make_async_copy(src, saves[name].at[layer], save_sem.at[k])

    pending = {}

    def start_save(name, layer, src):
        k = list(saves).index(name)
        copy = save(name, layer, src, k)
        copy.start()
        pending[name] = copy

    def end_save(*names):
        for name in names:
            if name in pending:
                pending.pop(name).wait()

    def block(i):
        return pl.ds(pl.multiple_of(i * SEQ, SEQ), SEQ)

    def part(e, k):
        return remote(send.at[e], recv.at[e, k % 2], (p_send.at[e], p_recv.at[e]), k, core_id)

    sent = {}

    def send_part(e, k):
        sent[e] = part(e, k)
        sent[e].start()

    width = proj_st.shape[2] // 3
    heads = width // HEAD

    def attn_part(e, s, w, x_low, i, layer):
        b = (bias, far_bias)[s]
        r = block(i)
        proj = (mm_nt(x_low, w[: 3 * width, :]) + b[e * 4 + layer : e * 4 + layer + 1, : 3 * width]).astype(BF)
        visible = lax.broadcasted_iota(jnp.int32, (1, SEQ), 1) < meta[e * nc + i]
        mixed = []
        for h in range(heads):
            queries = proj[:, h * HEAD : (h + 1) * HEAD]
            keys = proj[:, width + h * HEAD : width + (h + 1) * HEAD]
            values = proj[:, 2 * width + h * HEAD : 2 * width + (h + 1) * HEAD]
            scores = jnp.where(visible, mm_nt(queries, keys) * SCALE, FILL)
            ex = jnp.exp(scores - jnp.max(scores, axis=1, keepdims=True))
            probs = (ex * (1.0 / jnp.sum(ex, axis=1, keepdims=True))).astype(BF)
            if e == 0:
                probs_st[s, i, h] = probs
            mixed.append(mm(probs, values).astype(BF))
        mixed = jnp.concatenate(mixed, axis=1)
        if e == 0:
            proj_st[s, r, :] = proj
            mixed_st[s, r, :] = mixed
        return mm(mixed, w[3 * width : 4 * width, :])

    def ffn_part(e, s, w, x_low, i, layer):
        b = (bias, far_bias)[s]
        r = block(i)
        u = mm(x_low, w[0]) + b[e * 4 + 2 + layer : e * 4 + 3 + layer, :]
        portion = 0.5 + 0.5 * lax.erf(u * (0.5**0.5))
        active = (u * portion).astype(BF)
        if e == 0:
            active_st[s, r, :] = active
            slope_st[s, r, :] = (
                portion + u * (jnp.exp(-0.5 * u * u) * ((2 * math.pi) ** -0.5))
            ).astype(BF)
        return mm(active, w[1])

    def crops(body):
        lax.fori_loop(0, nc, lambda i, _: (body(i), 0)[1], 0)

    def joined(e, k, r):
        return base[e, r, :] + (send[e, r, :].astype(F32) + recv[e, k % 2, r, :].astype(F32))

    def attn_own(e, layer):
        for copy in load_a(e, layer):
            copy.wait()
        if layer == 0:
            x_local[e].wait()
            x_remote[e].wait_recv()
        else:
            part(e, 2 * layer - 1).wait_recv()
        if e == 0:
            end_save("v1", "normed", "proj", "probs", "mixed")

        def body(i):
            r = block(i)
            if layer == 0:
                x_low = low[e, r, :]
                x = x_low.astype(F32)
            else:
                v = joined(e, 2 * layer - 1, r)
                if e == 0:
                    v_st[r, :] = v
                x = norm(v, gains[e][layer - 1, 1:2, :], shifts[e][layer - 1, 3:4, :])[2]
                x_low = x.astype(BF)
                low[e, r, :] = x_low
            base[e, r, :] = x + shifts[e][layer, 0:1, :]
            acc[e, r, :] = attn_part(e, 0, own_a.at[e], x_low, i, layer)

        crops(body)
        if layer + 1 < LAYERS:
            for copy in load_a(e, layer + 1):
                copy.start()
        if e == 0:
            start_save("hidden", layer, low.at[e])
            if layer > 0:
                start_save("v2", layer - 1, v_st)

    def attn_far(e, layer):
        if e in sent:
            sent[e].wait_send()

        def body(i):
            r = block(i)
            total = acc[e, r, :] + attn_part(e, 1, far.at[2 * layer + e, 0], low[e, r, :], i, layer)
            send[e, r, :] = total.astype(BF)

        crops(body)
        send_part(e, 2 * layer)
        if e == 0:
            start_save("proj", layer, proj_st)
            start_save("probs", layer, probs_st)
            start_save("mixed", layer, mixed_st)

    def ffn_own(e, layer):
        for copy in load_f(e, layer):
            copy.wait()
        part(e, 2 * layer).wait_recv()
        if e == 0:
            end_save("hidden", "v2", "active", "slope")

        def body(i):
            r = block(i)
            v = joined(e, 2 * layer, r)
            if e == 0:
                v_st[r, :] = v
            x = norm(v, gains[e][layer, 0:1, :], shifts[e][layer, 1:2, :])[2]
            x_low = x.astype(BF)
            low[e, r, :] = x_low
            base[e, r, :] = x + shifts[e][layer, 2:3, :]
            acc[e, r, :] = ffn_part(e, 0, own_f.at[e], x_low, i, layer)

        crops(body)
        if layer + 1 < LAYERS:
            for copy in load_f(e, layer + 1):
                copy.start()
        if e == 0:
            start_save("normed", layer, low.at[e])
            start_save("v1", layer, v_st)

    def ffn_far(e, layer):
        sent[e].wait_send()

        def body(i):
            r = block(i)
            total = acc[e, r, :] + ffn_part(
                e, 1, far.at[2 * layer + e, pl.ds(1, 2)], low[e, r, :], i, layer
            )
            send[e, r, :] = total.astype(BF)

        crops(body)
        send_part(e, 2 * layer + 1)
        if e == 0:
            start_save("active", layer, active_st)
            start_save("slope", layer, slope_st)

    def pool(e):
        part(e, 2 * LAYERS - 1).wait_recv()
        if e == 0:
            end_save("v1")

        def body(i):
            r = block(i)
            v = joined(e, 2 * LAYERS - 1, r)
            if e == 0:
                v_st[r, :] = v
            x = norm(v, gains[e][LAYERS - 1, 1:2, :], shifts[e][LAYERS - 1, 3:4, :])[2]
            visible = lax.broadcasted_iota(jnp.int32, (SEQ, 1), 0) < meta[e * nc + i]
            sums[e, pl.ds(i, 1), :] = rows(jnp.where(visible, x, 0.0))

        crops(body)
        if e == 0:
            start_save("v2", LAYERS - 1, v_st)

    far_copies = []

    def keep_far(g):
        layer, e, kind = order[g]
        if e == 0:
            src = (far.at[2 * layer, 0:1], far.at[2 * layer, 1:3])[kind]
            dst = (far_out.at[layer, 0:1], far_out.at[layer, 1:3])[kind]
            copy = pltpu.make_async_copy(src, dst, save_sem.at[9 + 2 * layer + kind])
            copy.start()
            far_copies.append(copy)

    AO, AF, FO, FF = attn_own, attn_far, ffn_own, ffn_far
    P1, P2 = pass_first, pass_second

    def P3(g):
        ready(g)
        keep_far(g)

    AO(0, 0)
    P1(0)
    AO(1, 0)
    P1(1)
    P2(0)
    P3(0)
    b_copy.wait_recv()
    AF(0, 0)
    P2(1)
    P3(1)
    AF(1, 0)
    P1(2)
    FO(0, 0)
    FO(1, 0)
    P2(2)
    P1(3)
    P3(2)
    FF(0, 0)
    P1(4)
    AO(0, 1)
    P2(3)
    P3(3)
    FF(1, 0)
    P1(5)
    P2(4)
    P3(4)
    AF(0, 1)
    AO(1, 1)
    P1(6)
    P2(5)
    P3(5)
    AF(1, 1)
    FO(0, 1)
    FO(1, 1)
    P1(7)
    P2(6)
    P3(6)
    FF(0, 1)
    P2(7)
    P3(7)
    FF(1, 1)
    pool(0)
    pool(1)
    contrast(dp_size, nc, d, half, bit_ids, count, inv_q, inv_k, sums, pair_out, grad_out, held, c_send, c_recv, remote)
    end_save(*saves)
    for copy in far_copies:
        copy.wait()
    for e in range(2):
        sent[e].wait_send()
        x_remote[e].wait_send()
    b_copy.wait_send()
    for made, _, kind in moves:
        for copy in made.values():
            copy.wait_send()


def flips(dp_size, with_core):
    d = lax.axis_index("dp")
    t = lax.axis_index("tensor")
    found = [(d, t ^ 2)]
    for b in range(dp_size.bit_length() - 1):
        found.append((d ^ (1 << b), t))
    if with_core:
        found.append((d, t ^ 1))
    return found


def greet(partners):
    barrier = pltpu.get_barrier_semaphore()
    for p in partners:
        pl.semaphore_signal(barrier, inc=1, device_id=p, device_id_type=MESH)
    pl.semaphore_wait(barrier, len(partners))


def contrast(
    dp_size, nc, d, half, bit_ids, count, inv_q, inv_k, sums, pair_out, grad_out, held, send, recv, remote
):
    wide = D + 128
    dp_bits = dp_size.bit_length() - 1
    low = jnp.int32(0)
    for k in range(dp_bits):
        low = low + (((d >> (dp_bits - 1 - k)) & 1) << k)
    me = low + half * dp_size

    def unit(s, inv):
        pooled = s * inv
        r = lax.rsqrt(jnp.sum(pooled * pooled, axis=1, keepdims=True) + EPS)
        return pooled * r, r

    unit_q, rate_q = unit(sums[0, 0:nc, :], inv_q[...])
    unit_k, _ = unit(sums[1, 0:nc, :], inv_k[...])
    held[me] = jnp.zeros((8, wide), F32)
    held[me, 0:nc, 0:D] = unit_k
    held[me, nc : 2 * nc, 0:D] = unit_q
    slot = half * nc + lax.broadcasted_iota(jnp.int32, (nc, 128), 0)
    lane = lax.broadcasted_iota(jnp.int32, (nc, 128), 1)
    held[me, 0:nc, D:wide] = jnp.where((slot < count[0]) & (lane == 0), 1.0, 0.0)
    for s, p in enumerate(bit_ids):
        mine = pl.ds((me >> s) << s, 1 << s)
        theirs = pl.ds(((me >> s) ^ 1) << s, 1 << s)
        remote(held.at[mine], held.at[mine], (send, recv), s, p).start()
        remote(held.at[theirs], held.at[theirs], (send, recv), s, p).wait_recv()
    for s, p in enumerate(bit_ids):
        mine = pl.ds((me >> s) << s, 1 << s)
        remote(held.at[mine], held.at[mine], (send, recv), s, p).wait_send()
    chips = held.shape[0]
    every = held[...].reshape(chips * 8, wide)
    keys = every[:, 0:D]
    here = jnp.concatenate([held[low], held[low + dp_size]], axis=0)[:, 0:D]

    def exact(a, b, dims):
        return lax.dot_general(
            a, b, (dims, ((), ())), precision=lax.Precision.HIGHEST, preferred_element_type=F32
        )

    one = jnp.where(lax.broadcasted_iota(jnp.int32, (16, 128), 1) == 0, 1.0, 0.0)
    live = exact(one, every[:, D:wide], ((1,), (1,))) > 0.5
    logits = exact(here, keys, ((1,), (1,))) / TEMPER
    masked = jnp.where(live, logits, FILL)
    highest = jnp.max(masked, axis=1, keepdims=True)
    e = jnp.exp(masked - highest)
    total = jnp.sum(e, axis=1, keepdims=True)
    row = lax.broadcasted_iota(jnp.int32, (16, 1), 0)
    chip = row // 8
    place = row % 8 - nc
    column = lax.broadcasted_iota(jnp.int32, (16, chips * 8), 1)
    own = column == (low + chip * dp_size) * 8 + place
    live_here = (place >= 0) & (place < nc) & (chip * nc + place < count[0])
    own_logit = jnp.sum(jnp.where(own, logits, 0.0), axis=1, keepdims=True)
    pair_out[...] = jnp.broadcast_to(
        jnp.where(live_here, highest + jnp.log(total) - own_logit, 0.0), (16, 128)
    )
    weighting = jnp.where(live_here, e / total - own.astype(F32), 0.0) * (SEQ / TEMPER)
    g_unit = exact(weighting, keys, ((1,), (0,)))
    g_unit = jnp.where(half == 0, g_unit[nc : 2 * nc], g_unit[8 + nc : 8 + 2 * nc])
    g_pooled = rate_q * (g_unit - unit_q * jnp.sum(unit_q * g_unit, axis=1, keepdims=True))
    grad_out[...] = g_pooled * inv_q[...]


def total_over(dp_size, v_ref, out_ref, held, got, send, recv):
    partners = flips(dp_size, True)
    greet(partners)
    held[0] = v_ref[...]
    for s, p in enumerate(partners):
        copy = pltpu.make_async_remote_copy(
            src_ref=held.at[s],
            dst_ref=got.at[s],
            send_sem=send.at[s],
            recv_sem=recv.at[s],
            device_id=p,
            device_id_type=MESH,
        )
        copy.start()
        copy.wait()
        held[s + 1] = held[s] + got[s]
    out_ref[...] = held[len(partners)]


def ffn_backward(top, meta, *refs):
    refs = list(refs)
    if top:
        g_sum = refs.pop(0)
    else:
        base, theirs = [refs.pop(0) for _ in range(2)]
    v, slope, own_in, own_down, far_in, far_down, gain = [refs.pop(0) for _ in range(7)]
    base_out, part_out, low_out, inner_out, vec_out, bias_out = refs
    crop = pl.program_id(0)

    @pl.when(crop == 0)
    def _():
        vec_out[...] = jnp.zeros_like(vec_out)
        bias_out[...] = jnp.zeros_like(bias_out)

    if top:
        visible = lax.broadcasted_iota(jnp.int32, (SEQ, 1), 0) < meta[crop]
        g = jnp.where(visible, g_sum[0], 0.0)
    else:
        g = base[...] + theirs[...].astype(F32)
    xh, rate, _ = norm(v[0], gain[1:2, :], 0.0)
    gc = norm_back(g, xh, rate, gain[1:2, :])
    vec_out[0:1, :] += rows(g * xh)
    vec_out[1:2, :] += rows(g)
    vec_out[2:3, :] += rows(gc)
    low = gc.astype(BF)
    low_out[...] = low
    part = None
    for s, (w_in, w_down) in enumerate(((own_in, own_down), (far_in, far_down))):
        w_in, w_down = [w[0] if len(w.shape) == 3 else w[0, 0] for w in (w_in, w_down)]
        inner = (mm_nt(low, w_down) * slope[0, s].astype(F32)).astype(BF)
        inner_out[s] = inner
        bias_out[s : s + 1, :] += rows(inner.astype(F32))
        term = mm_nt(inner, w_in)
        part = term if part is None else part + term
    base_out[...] = gc + part
    part_out[...] = part.astype(BF)


def attn_backward(meta, *refs):
    base, theirs, v, proj, probs, own, far, gain = refs[:8]
    base_out, part_out, low_out, proj_out, vec_out, bias_out = refs[8:]
    crop = pl.program_id(0)

    @pl.when(crop == 0)
    def _():
        vec_out[...] = jnp.zeros_like(vec_out)
        bias_out[...] = jnp.zeros_like(bias_out)

    g = base[...] + theirs[...].astype(F32)
    xh, rate, _ = norm(v[0], gain[0:1, :], 0.0)
    gr = norm_back(g, xh, rate, gain[0:1, :])
    vec_out[0:1, :] += rows(g * xh)
    vec_out[1:2, :] += rows(g)
    vec_out[2:3, :] += rows(gr)
    low = gr.astype(BF)
    low_out[...] = low
    width = proj.shape[3] // 3
    heads = width // HEAD
    part = None
    for s, w in enumerate((own[0], far[0, 0])):
        g_mixed = mm_nt(low, w[3 * width : 4 * width, :]).astype(BF)
        pr = proj[0, s]
        parts = [[], [], []]
        for h in range(heads):
            queries = pr[:, h * HEAD : (h + 1) * HEAD]
            keys = pr[:, width + h * HEAD : width + (h + 1) * HEAD]
            values = pr[:, 2 * width + h * HEAD : 2 * width + (h + 1) * HEAD]
            gm = g_mixed[:, h * HEAD : (h + 1) * HEAD]
            p_low = probs[0, s, 0, h]
            p = p_low.astype(F32)
            gp = mm_nt(gm, values)
            gs = (p * (gp - jnp.sum(p * gp, axis=1, keepdims=True))).astype(BF)
            parts[0].append((mm(gs, keys) * SCALE).astype(BF))
            parts[1].append((mm_tn(gs, queries) * SCALE).astype(BF))
            parts[2].append(mm_tn(p_low, gm).astype(BF))
        g_proj = jnp.concatenate(parts[0] + parts[1] + parts[2], axis=1)
        proj_out[s] = g_proj
        bias_out[s : s + 1, :] += rows(g_proj.astype(F32))
        term = mm(g_proj, w[: 3 * width, :])
        part = term if part is None else part + term
    base_out[...] = gr + part
    part_out[...] = part.astype(BF)


def ffn_weights(low, active, normed, inner, in_out, down_out):
    down_out[0] = mm_tn(low[...], active[0, 0])
    in_out[0] = mm_tn(normed[0], inner[0])


def attn_weights(low, mixed, hidden, g_proj, out):
    width = mixed.shape[3]
    out[0, :, 0 : 3 * width] = mm_tn(hidden[0], g_proj[0])
    out[0, :, 3 * width : 4 * width] = mm_tn(low[...], mixed[0, 0])


SMEM = pl.BlockSpec(memory_space=pltpu.SMEM)


def row_block(width):
    return pl.BlockSpec((SEQ, width), lambda i: (i, 0))


def shard_block(width):
    return pl.BlockSpec((2, SEQ, width), lambda i: (0, i, 0))


def whole_block(shape):
    return pl.BlockSpec(shape, lambda i: (0,) * len(shape))


def call(body, grid, ins, outs, scratch, flops, name):
    arrays = [a for a, _ in ins]
    size = sum(a.size * a.dtype.itemsize for a in arrays)
    size += sum(math.prod(s) * jnp.dtype(t).itemsize for s, t, _ in outs)
    return pl.pallas_call(
        body,
        grid=grid,
        in_specs=[s for _, s in ins],
        out_specs=[s for _, _, s in outs],
        out_shape=[jax.ShapeDtypeStruct(s, t) for s, t, _ in outs],
        scratch_shapes=scratch,
        compiler_params=pltpu.CompilerParams(vmem_limit_bytes=52 * MIB),
        cost_estimate=pl.CostEstimate(flops=int(flops), bytes_accessed=int(size), transcendentals=0),
        name=name,
    )(*arrays)


def on_device(mesh_shape, *args):
    (
        query_input,
        key_input,
        query_length,
        key_length,
        pair_count,
    ) = args[:5]
    encoders = (args[5:13], args[13:21])
    dp_size = mesh_shape["dp"]
    dp_bits = dp_size.bit_length() - 1
    d_pos = lax.axis_index("dp")
    t_pos = lax.axis_index("tensor")
    quarter = d_pos & 3
    core = t_pos & 1
    half = t_pos // 2
    share = query_input.shape[0]
    total_rows = 2 * share
    nc = total_rows // SEQ
    width = args[5].shape[3]

    def far_perm(x):
        return lax.ppermute(x, "tensor", [(i, i ^ 2) for i in range(4)])

    def core_perm(x):
        return lax.ppermute(x, "tensor", [(i, i ^ 1) for i in range(4)])

    def dp_perm(x, bit):
        return lax.ppermute(x, "dp", [(i, i ^ (1 << bit)) for i in range(dp_size)])

    blob_a = [
        jnp.concatenate(
            [w[0].transpose(0, 2, 3, 1).reshape(LAYERS, 3 * width, D), w[2]], axis=1
        )
        for w in encoders
    ]
    bias_rows = []
    for w in encoders:
        zero = jnp.zeros((LAYERS, width), F32)
        bias_rows += [jnp.concatenate([w[1][:, 0], zero, w[1][:, 1], zero], axis=1), w[4]]
    bias = jnp.concatenate(bias_rows, axis=0)
    lengths = [
        lax.dynamic_slice(v, (half * nc,), (nc,)) for v in (query_length, key_length)
    ]
    meta = jnp.concatenate(lengths)
    inverse = [(1.0 / v.astype(F32))[:, None] for v in lengths]
    grid = (nc,)
    gspec = whole_block((2, D))
    flat = row_block(D)
    big = (total_rows, D)
    heads = width // HEAD
    unit_flops = 2 * total_rows * D
    vmem = pl.BlockSpec(memory_space=pltpu.VMEM)
    hbm = pl.BlockSpec(memory_space=pl.ANY)
    hops = dp_bits + 1
    n_groups = 4 * LAYERS
    shaped = jax.ShapeDtypeStruct
    sem = pltpu.SemaphoreType.DMA
    rows_of = lambda *s: (LAYERS,) + s
    results = pl.pallas_call(
        functools.partial(forward, dp_size, nc),
        in_specs=[SMEM] * 2 + [hbm] * 8 + [vmem] * 7,
        out_specs=[hbm] * 10 + [vmem] * 2,
        out_shape=[
            shaped(rows_of(total_rows, D), BF),
            shaped(rows_of(2, total_rows, 3 * width), BF),
            shaped(rows_of(2, nc, heads, SEQ, SEQ), BF),
            shaped(rows_of(2, total_rows, width), BF),
            shaped(rows_of(total_rows, D), F32),
            shaped(rows_of(total_rows, D), BF),
            shaped(rows_of(2, total_rows, BLOB), BF),
            shaped(rows_of(2, total_rows, BLOB), BF),
            shaped(rows_of(total_rows, D), F32),
            shaped(rows_of(3, BLOB, D), BF),
            shaped((16, 128), F32),
            shaped((nc, D), F32),
        ],
        scratch_shapes=[
            pltpu.VMEM((2,) + big, BF),
            pltpu.VMEM((2,) + big, F32),
            pltpu.VMEM((2,) + big, F32),
            pltpu.VMEM((2,) + big, BF),
            pltpu.VMEM((2, 2) + big, BF),
            pltpu.VMEM((2, BLOB, D), BF),
            pltpu.VMEM((2, 2, BLOB, D), BF),
            pltpu.VMEM((2 * LAYERS, 3, BLOB, D), BF),
            pltpu.VMEM(big, F32),
            pltpu.VMEM((2, total_rows, 3 * width), BF),
            pltpu.VMEM((2, nc, heads, SEQ, SEQ), BF),
            pltpu.VMEM((2, total_rows, width), BF),
            pltpu.VMEM((2, total_rows, BLOB), BF),
            pltpu.VMEM((2, total_rows, BLOB), BF),
            pltpu.VMEM(bias.shape, F32),
            pltpu.VMEM((2, 8, D), F32),
            pltpu.VMEM((2 * dp_size, 8, D + 128), F32),
            sem((n_groups, 8)),
            sem((n_groups, 8)),
            sem((2, 2 * LAYERS)),
            sem((2, 2 * LAYERS)),
            sem((2,)),
            sem((2,)),
            sem((2, 4)),
            sem((9 + 2 * LAYERS,)),
            sem((hops,)),
            sem((hops,)),
            sem((2,)),
        ],
        compiler_params=pltpu.CompilerParams(
            collective_id=0, has_side_effects=True, vmem_limit_bytes=int(60.5 * MIB)
        ),
        cost_estimate=pl.CostEstimate(
            flops=unit_flops * 80 * BLOB // 4, bytes_accessed=100 * MIB, transcendentals=0
        ),
        name="forward",
    )(
        meta,
        pair_count,
        query_input,
        key_input,
        *blob_a,
        encoders[0][3],
        encoders[1][3],
        encoders[0][5],
        encoders[1][5],
        encoders[0][6],
        encoders[1][6],
        encoders[0][7],
        encoders[1][7],
        bias,
        *inverse,
    )
    kept = dict(
        zip(("hidden", "proj", "probs", "mixed", "v1", "normed", "active", "slope", "v2"), results)
    )
    far, pair_rows, g_sum = results[9:]
    per_pair = jnp.concatenate([pair_rows[nc : 2 * nc, 0], pair_rows[8 + nc : 8 + 2 * nc, 0]])

    def scatter(full, order):
        cur = full.reshape((2,) + (2,) * dp_bits + (D // dp_size, BLOB))
        axes = ["y"] + list(reversed(range(dp_bits)))
        for name in order:
            at = axes.index(name)
            bit = jnp.int32(0) if name == "y" else (d_pos >> name) & 1
            keep = lax.dynamic_index_in_dim(cur, bit, at, keepdims=False)
            send = lax.dynamic_index_in_dim(cur, 1 - bit, at, keepdims=False)
            got = far_perm(send) if name == "y" else dp_perm(send, name)
            cur = keep + got
            axes.pop(at)
        return cur

    rest = list(range(2, dp_bits))
    order_in = ["y", 0, 1] + rest
    order_down = [0, "y", 1] + rest
    order_attn = [1, "y", 0] + rest

    vec_spec = whole_block((8, D))
    grad_in = [None] * LAYERS
    grad_down = [None] * LAYERS
    grad_attn = [None] * LAYERS
    vectors = [None] * LAYERS
    g_state = None
    for layer in reversed(range(LAYERS)):
        w = encoders[0]
        gains = w[6]
        top = layer == LAYERS - 1

        def layer_rows(dims, kind):
            if kind == 0:
                return pl.BlockSpec((1, SEQ, dims), lambda i: (layer, i, 0))
            return pl.BlockSpec((1, 2, SEQ, dims), lambda i: (layer, 0, i, 0))

        own_spec = pl.BlockSpec((1, BLOB, D), lambda i: (layer, 0, 0))
        far_specs = [pl.BlockSpec((1, 1, BLOB, D), lambda i, k=k: (layer, k, 0, 0)) for k in range(3)]
        ins = [(meta, SMEM)]
        if top:
            ins += [(g_sum.reshape(nc, 1, D), pl.BlockSpec((1, 1, D), lambda i: (i, 0, 0)))]
        else:
            ins += [(a, flat) for a in g_state]
        ins += [(kept["v2"], layer_rows(D, 0)), (kept["slope"], layer_rows(BLOB, 1))]
        ins += [(w[3], own_spec), (w[5], own_spec), (far, far_specs[1]), (far, far_specs[2])]
        ins += [(gains[layer], gspec)]
        base, part, low, inner, vec_f, bias_f = call(
            functools.partial(ffn_backward, top),
            grid,
            ins,
            [
                (big, F32, flat),
                (big, BF, flat),
                (big, BF, flat),
                ((2, total_rows, BLOB), BF, shard_block(BLOB)),
                ((8, D), F32, vec_spec),
                ((8, BLOB), F32, whole_block((8, BLOB))),
            ],
            [],
            unit_flops * 4 * BLOB,
            f"ffn_backward_{layer}",
        )
        other = core_perm(part)
        one_shard = pl.BlockSpec((1, total_rows, BLOB), lambda i: (i, 0, 0))
        full_out = pl.BlockSpec((1, D, BLOB), lambda i: (i, 0, 0))
        layer_whole = pl.BlockSpec((1,) + big, lambda i: (layer, 0, 0))

        def layer_shard(dims):
            return pl.BlockSpec((1, 1, total_rows, dims), lambda i: (layer, i, 0, 0))

        g_in, g_down = call(
            ffn_weights,
            (2,),
            [
                (low, whole_block(big)),
                (kept["active"], layer_shard(BLOB)),
                (kept["normed"], layer_whole),
                (inner, one_shard),
            ],
            [((2, D, BLOB), F32, full_out), ((2, D, BLOB), F32, full_out)],
            [],
            unit_flops * 4 * BLOB,
            f"ffn_weights_{layer}",
        )
        grad_in[layer] = scatter(g_in, order_in)
        grad_down[layer] = scatter(g_down, order_down)
        ins = [(meta, SMEM), (base, flat), (other, flat)]
        ins += [(kept["v1"], layer_rows(D, 0)), (kept["proj"], layer_rows(3 * width, 1))]
        ins += [
            (kept["probs"], pl.BlockSpec((1, 2, 1, heads, SEQ, SEQ), lambda i: (layer, 0, i, 0, 0, 0)))
        ]
        ins += [(blob_a[0], own_spec), (far, far_specs[0]), (gains[layer], gspec)]
        base, part, low, g_proj, vec_a, bias_a = call(
            attn_backward,
            grid,
            ins,
            [
                (big, F32, flat),
                (big, BF, flat),
                (big, BF, flat),
                ((2, total_rows, 3 * width), BF, shard_block(3 * width)),
                ((8, D), F32, vec_spec),
                ((8, 3 * width), F32, whole_block((8, 3 * width))),
            ],
            [],
            unit_flops * 14 * width,
            f"attn_backward_{layer}",
        )
        if layer > 0:
            g_state = (base, core_perm(part))
        else:
            mine = lax.dynamic_slice(base, (core * share, 0), (share, D))
            away = lax.dynamic_slice(part, ((1 - core) * share, 0), (share, D))
            query_grad = mine + core_perm(away).astype(F32)
        (g_attn,) = call(
            attn_weights,
            (2,),
            [
                (low, whole_block(big)),
                (kept["mixed"], layer_shard(width)),
                (kept["hidden"], layer_whole),
                (g_proj, pl.BlockSpec((1, total_rows, 3 * width), lambda i: (i, 0, 0))),
            ],
            [((2, D, BLOB), F32, full_out)],
            [],
            unit_flops * 8 * width,
            f"attn_weights_{layer}",
        )
        grad_attn[layer] = scatter(g_attn, order_attn)
        vectors[layer] = (vec_f, bias_f, vec_a, bias_a)

    first = jnp.where(core == 0, 1.0, 0.0)
    packed = []
    for vec_f, bias_f, vec_a, bias_a in vectors:
        norms = jnp.stack([vec_a[0], vec_f[0], vec_a[2], vec_a[1], vec_f[2], vec_f[1]]) * first
        inner_rows = jnp.zeros((4, BLOB), F32)
        inner_rows = lax.dynamic_update_slice(inner_rows, bias_f[0:1], (t_pos, 0))
        inner_rows = lax.dynamic_update_slice(inner_rows, bias_f[1:2], (t_pos ^ 2, 0))
        qv = jnp.zeros((4, 2, width), F32)
        for s, at in ((0, t_pos), (1, t_pos ^ 2)):
            both = jnp.stack([bias_a[s, :width], bias_a[s, 2 * width :]])
            qv = lax.dynamic_update_slice(qv, both[None], (at, 0, 0))
        packed.append(jnp.concatenate([norms, inner_rows, qv.transpose(1, 0, 2).reshape(2, 4 * width)]))
    packed = jnp.concatenate(packed)
    hops += 1
    summed = pl.pallas_call(
        functools.partial(total_over, dp_size),
        in_specs=[vmem],
        out_specs=vmem,
        out_shape=jax.ShapeDtypeStruct(packed.shape, F32),
        scratch_shapes=[
            pltpu.VMEM((hops + 1,) + packed.shape, F32),
            pltpu.VMEM((hops,) + packed.shape, F32),
            pltpu.SemaphoreType.DMA((hops,)),
            pltpu.SemaphoreType.DMA((hops,)),
        ],
        compiler_params=pltpu.CompilerParams(
            collective_id=1, has_side_effects=True, vmem_limit_bytes=16 * MIB
        ),
        name="total_over",
    )(packed)
    summed = summed.reshape(LAYERS, 12, D)
    grad_gain = summed[:, 0:2]
    grad_shift = summed[:, 2:6]
    grad_in_bias = summed[:, 6:10].reshape(LAYERS, 4 * BLOB)
    grad_qv_bias = summed[:, 10:12]

    attn = jnp.stack(grad_attn)
    return (
        per_pair,
        query_grad,
        attn[:, :, : 3 * width].reshape(LAYERS, D // dp_size, 3, width),
        attn[:, :, 3 * width :].transpose(0, 2, 1),
        jnp.stack(grad_in),
        jnp.stack(grad_down).transpose(0, 2, 1),
        grad_qv_bias,
        grad_in_bias,
        grad_gain,
        grad_shift,
    )


def solution(mesh):
    split = P(("dp", "tensor"), None)
    weights = (
        P(None, None, None, "tensor"),
        P(None, None, "tensor"),
        P(None, "tensor", None),
        P(None, None, "tensor"),
        P(None, "tensor"),
        P(None, "tensor", None),
        P(),
        P(),
    )
    return jax.shard_map(
        functools.partial(on_device, dict(mesh.shape)),
        mesh=mesh,
        in_specs=(split, split, P("dp"), P("dp"), P("dp")) + weights + weights,
        out_specs=(
            P("dp"),
            split,
            P(None, "dp", None, "tensor"),
            P(None, "tensor", "dp"),
            P(None, "dp", "tensor"),
            P(None, "tensor", "dp"),
            P(),
            P(),
            P(),
            P(),
        ),
        check_vma=False,
    )
```

time: 659 us -> 582 us (0.88)
  Pallas kernels: 265 us -> 328 us
  starting transfers between devices: 89.5 us -> 27.1 us
  waiting for transfers between devices: 178 us -> 133 us
  local copies, waits for them, and re-layouts: 71.4 us -> 46.7 us
    pallas_call x1, Pallas kernels: 19.9 us -> 182 us  [on_device(): pl.pallas_call(functools.partial(forward, dp_size, nc), in_specs=[SMEM] *...]
    pallas_call x18 -> x8, Pallas kernels: 182 us -> 84.5 us  [call(): pl.pallas_call(body, grid=grid, in_specs=[s for _, s in ins], out_specs=[...]
    ppermute x66 -> x18, waiting for transfers between devices: 152 us -> 123 us  [dp_perm(): return lax.ppermute(x, 'dp', [(i, i ^ 1 << bit) for i in range(dp_size)])]
    ppermute x66 -> x18, starting transfers between devices: 49.6 us -> 20.7 us  [dp_perm(): return lax.ppermute(x, 'dp', [(i, i ^ 1 << bit) for i in range(dp_size)])]
    ppermute x14 -> x4, starting transfers between devices: 23.7 us -> 2.54 us  [core_perm(): return lax.ppermute(x, 'tensor', [(i, i ^ 1) for i in range(4)])]
    ppermute x19 -> x6, waiting for transfers between devices: 25.5 us -> 9.66 us  [far_perm(): return lax.ppermute(x, 'tensor', [(i, i ^ 2) for i in range(4)])]
    slice x36 -> x2, local copies, waits for them, and re-layouts: 15.8 us -> 1.53 us  [on_device(): w[1][:, 0]]
    ppermute x19 -> x6, starting transfers between devices: 16.2 us -> 3.8 us  [far_perm(): return lax.ppermute(x, 'tensor', [(i, i ^ 2) for i in range(4)])]
  transfers between devices with their start and end apart: 99 -> 28, of which waited for: 29 -> 11; matrix products, arithmetic and copies ran while one was open for 15% -> 11% of each run, Pallas kernels for 35% -> 24%
where the time goes in v2:
time: 582 us; the launch traced here: 573 us
  Pallas kernels  328 us (56%)
  waiting for transfers between devices  133 us (23%)
  local copies, waits for them, and re-layouts  46.7 us (8%)
  other arithmetic  35.6 us (6%)
  starting transfers between devices  27.1 us (5%)
    pallas_call x1, Pallas kernels, on_device(): pl.pallas_call(functools.partial(forward, dp_size, nc), in_specs=[SMEM] *...  182 us
    ppermute x18, waiting for transfers between devices, dp_perm(): return lax.ppermute(x, 'dp', [(i, i ^ 1 << bit) for i in range(dp_size)])  123 us
    pallas_call x8, Pallas kernels, call(): pl.pallas_call(body, grid=grid, in_specs=[s for _, s in ins], out_specs=[...  84.5 us
    pallas_call x1, Pallas kernels, on_device(): pl.pallas_call(functools.partial(total_over, dp_size), in_specs=[vmem], o...  61.8 us
    add x18, other arithmetic, scatter(): cur = keep + got  23.2 us
    ppermute x18, starting transfers between devices, dp_perm(): return lax.ppermute(x, 'dp', [(i, i ^ 1 << bit) for i in range(dp_size)])  20.7 us
    squeeze x20, local copies, waits for them, and re-layouts, scatter(): send = lax.dynamic_index_in_dim(cur, 1 - bit, at, keepdims=False)  19.2 us
  transfers between devices with their start and end apart: 28, of which 11 were waited for; matrix products, arithmetic and copies ran while one was open for 11% of the time, Pallas kernels for 24%

profile of v2, /device:TPU:29, one launch (start us, length us, event | category | flops | bytes accessed | tf_op | source)
XLA Modules:
  0.0 573.0 jit_solution(7992729880701413128)
XLA Ops:
  6.3 4.0 pad_maximum_fusion
  10.9 182.1 %forward.1 = (bf16[2,768,768]{2,1,0:T(8,128)(2,1)}, bf16[2,2,768,576]{3,2,1,0:T(8,128)(2,1)}, bf16[2,2,3,3,256,256]{5,4,3,2,1,0:T(8,128)(2,1)}, bf16[2,2,768,192...) custom-call(s32[6]{0:T(128)} %pad_add_fusion.refs_0_.meta, ...), custom_call_target="tpu_custom_call" | custom-call | flops 18119393280 | bytes 104857600 | tf_op jit(solution)/shard_map/forward/pallas_call | solution.py:749
  193.7 10.9 %ffn_backward_1.1 = (f32[768,768]{1,0:T(8,128)}, bf16[768,768]{1,0:T(8,128)(2,1)S(1)}, bf16[768,768]{1,0:T(8,128)(2,1)}, bf16[2,768,768]{2,1,0:T(8,128)(2,1)}, f...) custom-call(s32[6]{0:T(128)S(1)} %copy-done.2, f32[3,1,768]{2,1,0:T(1,128)S(1)} %reshape.68.refs_0_, ...), custom_call_target="tpu_custom_call" | custom-call | flops 3623878656 | bytes 35453976 | tf_op jit(solution)/shard_map/ffn_backward_1/pallas_call | solution.py:677
  207.5 7.9 %ffn_weights_1.1 = (f32[2,768,768]{2,1,0:T(8,128)}, f32[2,768,768]{2,1,0:T(8,128)}) custom-call(bf16[768,768]{1,0:T(8,128)(2,1)S(1)} %copy-done.3, bf16[2,2,768,768]{3,2,1,0:T(8,128)(2,1)} %get-tuple-element.73.active, bf16[2,768,768]{2,1,0:T(8,128)(2,1)} %get-tuple-element.74.normed, bf16[2,768,768]{2,1,0:T(8,128)(2,1)} %get-tuple-element.78.inner), custom_call_target="tpu_custom_call" | custom-call | flops 3623878656 | bytes 20054016 | tf_op jit(solution)/shard_map/ffn_weights_1/pallas_call | solution.py:677
  215.4 3.4 dynamic-slice_bitcast_fusion
  218.8 2.5 fusion.13
  224.7 17.0 %attn_backward_1.1 = (f32[768,768]{1,0:T(8,128)}, bf16[768,768]{1,0:T(8,128)(2,1)S(1)}, bf16[768,768]{1,0:T(8,128)(2,1)}, bf16[2,768,576]{2,1,0:T(8,128)(2,1)}, ...) custom-call(s32[6]{0:T(128)S(1)} %copy-done.2, f32[768,768]{1,0:T(8,128)} %get-tuple-element.55.refs_0_, ...), custom_call_target="tpu_custom_call" | custom-call | flops 3170893824 | bytes 32489496 | tf_op jit(solution)/shard_map/attn_backward_1/pallas_call | solution.py:677
  243.3 6.2 %attn_weights_1.1 = f32[2,768,768]{2,1,0:T(8,128)} custom-call(bf16[768,768]{1,0:T(8,128)(2,1)S(1)} %copy-done.1, bf16[2,2,768,192]{3,2,1,0:T(8,128)(2,1)} %get-tuple-element.67.mixed, bf16[2,768,768]{2,1,0:T(8,128)(2,1)} %get-tuple-element.68.hidden, bf16[2,768,576]{2,1,0:T(8,128)(2,1)} %get-tuple-element.71.g_proj), custom_call_target="tpu_custom_call" | custom-call | flops 1811939328 | bytes 11206656 | tf_op jit(solution)/shard_map/attn_weights_1/pallas_call | solution.py:677
  249.5 3.3 dynamic-slice_bitcast_fusion.2
  256.2 11.2 %ffn_backward_0.1 = (f32[768,768]{1,0:T(8,128)}, bf16[768,768]{1,0:T(8,128)(2,1)S(1)}, bf16[768,768]{1,0:T(8,128)(2,1)}, bf16[2,768,768]{2,1,0:T(8,128)(2,1)}, f...) custom-call(s32[6]{0:T(128)S(1)} %copy-done.2, f32[768,768]{1,0:T(8,128)} %get-tuple-element.60.refs_0_, ...), custom_call_target="tpu_custom_call" | custom-call | flops 3623878656 | bytes 38983704 | tf_op jit(solution)/shard_map/ffn_backward_0/pallas_call | solution.py:677
  269.0 7.8 %ffn_weights_0.1 = (f32[2,768,768]{2,1,0:T(8,128)}, f32[2,768,768]{2,1,0:T(8,128)}) custom-call(bf16[768,768]{1,0:T(8,128)(2,1)S(1)} %copy-done.4, bf16[2,2,768,768]{3,2,1,0:T(8,128)(2,1)} %get-tuple-element.73.active, bf16[2,768,768]{2,1,0:T(8,128)(2,1)} %get-tuple-element.74.normed, bf16[2,768,768]{2,1,0:T(8,128)(2,1)} %get-tuple-element.75.inner), custom_call_target="tpu_custom_call" | custom-call | flops 3623878656 | bytes 20054016 | tf_op jit(solution)/shard_map/ffn_weights_0/pallas_call | solution.py:677
  276.8 3.2 dynamic-slice_bitcast_fusion.1
  280.0 2.7 bitcast_add_fusion.2
  284.6 4.9 fusion.12
  295.2 17.3 %attn_backward_0.1 = (f32[768,768]{1,0:T(8,128)}, bf16[768,768]{1,0:T(8,128)(2,1)S(1)}, bf16[768,768]{1,0:T(8,128)(2,1)}, bf16[2,768,576]{2,1,0:T(8,128)(2,1)}, ...) custom-call(s32[6]{0:T(128)S(1)} %copy-done.2, f32[768,768]{1,0:T(8,128)} %get-tuple-element.62.refs_0_, ...), custom_call_target="tpu_custom_call" | custom-call | flops 3170893824 | bytes 32489496 | tf_op jit(solution)/shard_map/attn_backward_0/pallas_call | solution.py:677
  313.1 61.8 %total_over.1 = f32[24,768]{1,0:T(8,128)S(1)} custom-call(f32[24,768]{1,0:T(8,128)S(1)} %concatenate.31.v_ref), custom_call_target="tpu_custom_call" | custom-call | tf_op jit(solution)/shard_map/total_over/pallas_call | solution.py:970
  381.8 2.7 bitcast_add_fusion
  385.7 6.1 %attn_weights_0.1 = f32[2,768,768]{2,1,0:T(8,128)} custom-call(bf16[768,768]{1,0:T(8,128)(2,1)S(1)} %copy-done, bf16[2,2,768,192]{3,2,1,0:T(8,128)(2,1)} %get-tuple-element.67.mixed, bf16[2,768,768]{2,1,0:T(8,128)(2,1)} %get-tuple-element.68.hidden, bf16[2,768,576]{2,1,0:T(8,128)(2,1)} %get-tuple-element.69.g_proj), custom_call_target="tpu_custom_call" | custom-call | flops 1811939328 | bytes 11206656 | tf_op jit(solution)/shard_map/attn_weights_0/pallas_call | solution.py:677
  391.8 3.3 dynamic-slice_bitcast_fusion.3
  399.1 6.9 %collective-permute-done.18 = f32[2,96,768]{2,1,0:T(8,128)} collective-permute-done((f32[2,96,768]{2,1,0:T(8,128)S(1)}, f32[2,96,768]{2,1,0:T(8,128)}, u32[]{:S(2)}, u32[]{:S(2)}) %collective-permute-start.18) | collective-permute-done | bytes 589856 | tf_op jit(solution)/shard_map/ppermute | solution.py:718
  408.5 3.0 collective-permute-start.27
  412.7 50.8 %collective-permute-done.27 = f32[96,768]{1,0:T(8,128)S(1)} collective-permute-done((f32[96,768]{1,0:T(8,128)S(1)}, f32[96,768]{1,0:T(8,128)S(1)}, u32[]{:S(2)}, u32[]{:S(2)}) %collective-permute-start.27) | collective-permute-done | bytes 294944 | tf_op jit(solution)/shard_map/ppermute | solution.py:718
  463.5 3.1 collective-permute-start.19
  471.7 8.2 %collective-permute-done.19 = f32[96,768]{1,0:T(8,128)S(1)} collective-permute-done((f32[96,768]{1,0:T(8,128)S(1)}, f32[96,768]{1,0:T(8,128)S(1)}, u32[]{:S(2)}, u32[]{:S(2)}) %collective-permute-start.19) | collective-permute-done | bytes 294944 | tf_op jit(solution)/shard_map/ppermute | solution.py:718
  487.1 2.7 bitcast_add_fusion.1
  490.0 6.7 %collective-permute-done.21 = f32[2,2,96,768]{3,2,1,0:T(8,128)} collective-permute-done((f32[2,2,96,768]{3,2,1,0:T(8,128)}, f32[2,2,96,768]{3,2,1,0:T(8,128)}, u32[]{:S(2)}, u32[]{:S(2)}) %collective-permute-start.21) | collective-permute-done | bytes 1179680 | tf_op jit(solution)/shard_map/ppermute | solution.py:712
  498.9 7.4 %collective-permute-done.11 = f32[96,768]{0,1:T(8,128)} collective-permute-done((f32[96,768]{0,1:T(8,128)}, f32[96,768]{0,1:T(8,128)}, u32[]{:S(2)}, u32[]{:S(2)}) %collective-permute-start.11) | collective-permute-done | bytes 294944 | tf_op jit(solution)/shard_map/ppermute | solution.py:718
  512.7 6.1 %collective-permute-done.22 = f32[2,96,768]{2,1,0:T(8,128)S(1)} collective-permute-done((f32[2,96,768]{2,1,0:T(8,128)S(1)}, f32[2,96,768]{2,1,0:T(8,128)S(1)}, u32[]{:S(2)}, u32[]{:S(2)}) %collective-permute-start.22) | collective-permute-done | bytes 589856 | tf_op jit(solution)/shard_map/ppermute | solution.py:718
  518.9 3.0 collective-permute-done.5
  522.4 15.3 %collective-permute-done.14 = f32[2,96,768]{2,1,0:T(8,128)S(1)} collective-permute-done((f32[2,96,768]{2,1,0:T(8,128)S(1)}, f32[2,96,768]{2,1,0:T(8,128)S(1)}, u32[]{:S(2)}, u32[]{:S(2)}) %collective-permute-start.14) | collective-permute-done | bytes 589856 | tf_op jit(solution)/shard_map/ppermute | solution.py:718
  541.3 21.1 %collective-permute-done.15 = f32[96,768]{1,0:T(8,128)} collective-permute-done((f32[96,768]{1,0:T(8,128)}, f32[96,768]{1,0:T(8,128)}, u32[]{:S(2)}, u32[]{:S(2)}) %collective-permute-start.15) | collective-permute-done | bytes 294944 | tf_op jit(solution)/shard_map/ppermute | solution.py:718
  565.2 5.5 collective-permute-done.7
  (196 shorter events, 72.6 us)
Async XLA Ops:
  10.9 182.8 %copy-start.2 = (s32[6]{0:T(128)S(1)}, s32[6]{0:T(128)}, u32[]{:S(2)}) copy-start(s32[6]{0:T(128)} %pad_add_fusion.refs_0_.meta) | copy-start | bytes 76
  204.7 19.0 %collective-permute-start = (bf16[768,768]{1,0:T(8,128)(2,1)S(1)}, bf16[768,768]{1,0:T(8,128)(2,1)S(1)}, u32[]{:S(2)}, u32[]{:S(2)}) collective-permute-start(bf16[768,768]{1,0:T(8,128)(2,1)S(1)} %get-tuple-element.56), channel_id=1, source_target_pairs={{0,1},{1,0},{2,3},{3,2},{4,5},{5,4},{6,7},{7,6},{8,9},{9,8},{10,11... | collective-permute-start | bytes 3538952 | tf_op jit(solution)/shard_map/ppermute | solution.py:715
  218.8 61.2 %collective-permute-start.24 = (f32[2,2,2,96,768]{4,3,2,1,0:T(8,128)}, f32[2,2,2,96,768]{4,3,2,1,0:T(8,128)}, u32[]{:S(2)}, u32[]{:S(2)}) collective-permute-start(f32[2,2,2,96,768]{4,3,2,1,0:T(8,128)} %dynamic-slice_bitcast_fusion), channel_id=1, source_target_pairs={{0,4},{4,0},{8,12},{12,8},{16,20},{20,16},{24,28},{28,24},{1,5},{5... | collective-permute-start | bytes 7077896 | tf_op jit(solution)/shard_map/ppermute | solution.py:718
  221.3 68.2 %collective-permute-start.16 = (f32[2,2,2,96,768]{4,3,2,1,0:T(8,128)}, f32[2,2,2,96,768]{4,3,2,1,0:T(8,128)}, u32[]{:S(2)}, u32[]{:S(2)}) collective-permute-start(f32[2,2,2,96,768]{4,3,2,1,0:T(8,128)} %bitcast.44), channel_id=1, source_target_pairs={{0,2},{1,3},{2,0},{3,1},{4,6},{5,7},{6,4},{7,5},{8,10},{9,11},{10,... | collective-permute-start | bytes 7077896 | tf_op jit(solution)/shard_map/ppermute | solution.py:712
  241.7 13.4 %collective-permute-start.1 = (bf16[768,768]{1,0:T(8,128)(2,1)S(1)}, bf16[768,768]{1,0:T(8,128)(2,1)S(1)}, u32[]{:S(2)}, u32[]{:S(2)}) collective-permute-start(bf16[768,768]{1,0:T(8,128)(2,1)S(1)} %get-tuple-element.61), channel_id=1, source_target_pairs={{0,1},{1,0},{2,3},{3,2},{4,5},{5,4},{6,7},{7,6},{8,9},{9,8},{10,11... | collective-permute-start | bytes 3538952 | tf_op jit(solution)/shard_map/ppermute | solution.py:715
  253.0 128.7 %collective-permute-start.8 = (f32[2,2,2,96,768]{4,3,2,1,0:T(8,128)}, f32[2,2,2,96,768]{4,3,2,1,0:T(8,128)}, u32[]{:S(2)}, u32[]{:S(2)}) collective-permute-start(f32[2,2,2,96,768]{4,3,2,1,0:T(8,128)} %dynamic-slice_bitcast_fusion.2), channel_id=1, source_target_pairs={{0,8},{4,12},{8,0},{12,4},{16,24},{20,28},{24,16},{28,20},{1,9},{5... | collective-permute-start | bytes 7077896 | tf_op jit(solution)/shard_map/ppermute | solution.py:718
  267.4 26.3 %collective-permute-start.2 = (bf16[768,768]{1,0:T(8,128)(2,1)S(1)}, bf16[768,768]{1,0:T(8,128)(2,1)S(1)}, u32[]{:S(2)}, u32[]{:S(2)}) collective-permute-start(bf16[768,768]{1,0:T(8,128)(2,1)S(1)} %get-tuple-element.63), channel_id=1, source_target_pairs={{0,1},{1,0},{2,3},{3,2},{4,5},{5,4},{6,7},{7,6},{8,9},{9,8},{10,11... | collective-permute-start | bytes 3538952 | tf_op jit(solution)/shard_map/ppermute | solution.py:715
  280.0 187.9 %collective-permute-start.20 = (f32[2,2,2,96,768]{4,3,2,1,0:T(8,128)}, f32[2,2,2,96,768]{4,3,2,1,0:T(8,128)}, u32[]{:S(2)}, u32[]{:S(2)}) collective-permute-start(f32[2,2,2,96,768]{4,3,2,1,0:T(8,128)} %dynamic-slice_bitcast_fusion.1), channel_id=1, source_target_pairs={{0,4},{4,0},{8,12},{12,8},{16,20},{20,16},{24,28},{28,24},{1,5},{5... | collective-permute-start | bytes 7077896 | tf_op jit(solution)/shard_map/ppermute | solution.py:718
  283.9 92.3 %collective-permute-start.25 = (f32[2,2,96,768]{3,2,1,0:T(8,128)}, f32[2,2,96,768]{3,2,1,0:T(8,128)}, u32[]{:S(2)}, u32[]{:S(2)}) collective-permute-start(f32[2,2,96,768]{3,2,1,0:T(8,128)} %slice_bitcast_fusion), channel_id=1, source_target_pairs={{0,2},{1,3},{2,0},{3,1},{4,6},{5,7},{6,4},{7,5},{8,10},{9,11},{10,... | collective-permute-start | bytes 3538952 | tf_op jit(solution)/shard_map/ppermute | solution.py:712
  289.5 190.4 %collective-permute-start.12 = (f32[2,2,2,96,768]{4,3,2,1,0:T(8,128)}, f32[2,2,2,96,768]{4,3,2,1,0:T(8,128)}, u32[]{:S(2)}, u32[]{:S(2)}) collective-permute-start(f32[2,2,2,96,768]{4,3,2,1,0:T(8,128)} %bitcast.35), channel_id=1, source_target_pairs={{0,2},{1,3},{2,0},{3,1},{4,6},{5,7},{6,4},{7,5},{8,10},{9,11},{10,... | collective-permute-start | bytes 7077896 | tf_op jit(solution)/shard_map/ppermute | solution.py:712
  293.7 86.1 %collective-permute-start.17 = (f32[2,2,96,768]{3,2,1,0:T(8,128)}, f32[2,2,96,768]{3,2,1,0:T(8,128)}, u32[]{:S(2)}, u32[]{:S(2)}) collective-permute-start(f32[2,2,96,768]{3,2,1,0:T(8,128)} %dynamic-slice_bitcast_fusion.4), channel_id=1, source_target_pairs={{0,4},{4,0},{8,12},{12,8},{16,20},{20,16},{24,28},{28,24},{1,5},{5... | collective-permute-start | bytes 3538952 | tf_op jit(solution)/shard_map/ppermute | solution.py:718
  378.2 18.3 %collective-permute-start.26 = (f32[2,96,768]{2,1,0:T(8,128)S(1)}, f32[2,96,768]{2,1,0:T(8,128)S(1)}, u32[]{:S(2)}, u32[]{:S(2)}) collective-permute-start(f32[2,96,768]{2,1,0:T(8,128)S(1)} %dynamic-slice_bitcast_fusion.6), channel_id=1, source_target_pairs={{0,8},{4,12},{8,0},{12,4},{16,24},{20,28},{24,16},{28,20},{1,9},{5... | collective-permute-start | bytes 1769480 | tf_op jit(solution)/shard_map/ppermute | solution.py:718
  381.3 24.7 %collective-permute-start.18 = (f32[2,96,768]{2,1,0:T(8,128)S(1)}, f32[2,96,768]{2,1,0:T(8,128)}, u32[]{:S(2)}, u32[]{:S(2)}) collective-permute-start(f32[2,96,768]{2,1,0:T(8,128)S(1)} %dynamic-slice_bitcast_fusion.8), channel_id=1, source_target_pairs={{0,8},{4,12},{8,0},{12,4},{16,24},{20,28},{24,16},{28,20},{1,9},{5... | collective-permute-start | bytes 1769480 | tf_op jit(solution)/shard_map/ppermute | solution.py:718
  384.6 82.1 %collective-permute-start.9 = (f32[2,2,96,768]{3,2,1,0:T(8,128)S(1)}, f32[2,2,96,768]{3,2,1,0:T(8,128)S(1)}, u32[]{:S(2)}, u32[]{:S(2)}) collective-permute-start(f32[2,2,96,768]{3,2,1,0:T(8,128)S(1)} %slice_bitcast_fusion.4), channel_id=1, source_target_pairs={{0,2},{1,3},{2,0},{3,1},{4,6},{5,7},{6,4},{7,5},{8,10},{9,11},{10,... | collective-permute-start | bytes 3538952 | tf_op jit(solution)/shard_map/ppermute | solution.py:712
  397.4 11.1 %collective-permute-start.3 = (bf16[384,768]{1,0:T(8,128)(2,1)S(1)}, bf16[384,768]{1,0:T(8,128)(2,1)S(1)}, u32[]{:S(2)}, u32[]{:S(2)}) collective-permute-start(bf16[384,768]{1,0:T(8,128)(2,1)S(1)} %constant_dynamic-slice_fusion.4), channel_id=1, source_target_pairs={{0,1},{1,0},{2,3},{3,2},{4,5},{5,4},{6,7},{7,6},{8,9},{9,8},{10,11... | collective-permute-start | bytes 1769480 | tf_op jit(solution)/shard_map/ppermute | solution.py:715
  397.8 70.1 %slice-start = ((s8[4718592]{0:T(1024)(128)(4,1)}), s8[4194304]{0:T(1024)(128)(4,1)S(1)}, s32[]{:S(2)}) async-start(s8[4718592]{0:T(1024)(128)(4,1)} %bitcast.181), calls=%async_computation | async-start | bytes 8388608
  406.1 81.1 %collective-permute-start.4 = (f32[2,2,2,96,768]{4,3,2,1,0:T(8,128)}, f32[2,2,2,96,768]{4,3,2,1,0:T(8,128)}, u32[]{:S(2)}, u32[]{:S(2)}) collective-permute-start(f32[2,2,2,96,768]{4,3,2,1,0:T(8,128)} %dynamic-slice_bitcast_fusion.3), channel_id=1, source_target_pairs={{0,8},{4,12},{8,0},{12,4},{16,24},{20,28},{24,16},{28,20},{1,9},{5... | collective-permute-start | bytes 7077896 | tf_op jit(solution)/shard_map/ppermute | solution.py:718
  408.5 55.0 %collective-permute-start.27 = (f32[96,768]{1,0:T(8,128)S(1)}, f32[96,768]{1,0:T(8,128)S(1)}, u32[]{:S(2)}, u32[]{:S(2)}) collective-permute-start(f32[96,768]{1,0:T(8,128)S(1)} %dynamic-slice_bitcast_fusion.12), channel_id=1, source_target_pairs={{0,16},{4,20},{8,24},{12,28},{16,0},{20,4},{24,8},{28,12},{1,17},{... | collective-permute-start | bytes 884744 | tf_op jit(solution)/shard_map/ppermute | solution.py:718
  411.6 56.3 %slice-start.1 = ((s8[4718592]{0:T(1024)(128)(4,1)}), s8[524288]{0:T(1024)(128)(4,1)S(1)}, s32[]{:S(2)}) async-start(s8[4718592]{0:T(1024)(128)(4,1)} %bitcast.181), calls=%async_computation.1 | async-start | bytes 1048576
  463.5 16.4 %collective-permute-start.19 = (f32[96,768]{1,0:T(8,128)S(1)}, f32[96,768]{1,0:T(8,128)S(1)}, u32[]{:S(2)}, u32[]{:S(2)}) collective-permute-start(f32[96,768]{1,0:T(8,128)S(1)} %dynamic-slice_bitcast_fusion.14), channel_id=1, source_target_pairs={{0,16},{4,20},{8,24},{12,28},{16,0},{20,4},{24,8},{28,12},{1,17},{... | collective-permute-start | bytes 884744 | tf_op jit(solution)/shard_map/ppermute | solution.py:718
  466.9 17.4 %collective-permute-start.10 = (f32[2,96,768]{2,1,0:T(8,128)S(1)}, f32[2,96,768]{2,1,0:T(8,128)S(1)}, u32[]{:S(2)}, u32[]{:S(2)}) collective-permute-start(f32[2,96,768]{2,1,0:T(8,128)S(1)} %dynamic-slice_bitcast_fusion.10), channel_id=1, source_target_pairs={{0,4},{4,0},{8,12},{12,8},{16,20},{20,16},{24,28},{28,24},{1,5},{5... | collective-permute-start | bytes 1769480 | tf_op jit(solution)/shard_map/ppermute | solution.py:718
  471.1 25.6 %collective-permute-start.21 = (f32[2,2,96,768]{3,2,1,0:T(8,128)}, f32[2,2,96,768]{3,2,1,0:T(8,128)}, u32[]{:S(2)}, u32[]{:S(2)}) collective-permute-start(f32[2,2,96,768]{3,2,1,0:T(8,128)} %slice_bitcast_fusion.2), channel_id=1, source_target_pairs={{0,2},{1,3},{2,0},{3,1},{4,6},{5,7},{6,4},{7,5},{8,10},{9,11},{10,... | collective-permute-start | bytes 3538952 | tf_op jit(solution)/shard_map/ppermute | solution.py:712
  483.1 26.0 %collective-permute-start.13 = (f32[2,2,96,768]{3,2,1,0:T(8,128)}, f32[2,2,96,768]{3,2,1,0:T(8,128)}, u32[]{:S(2)}, u32[]{:S(2)}) collective-permute-start(f32[2,2,96,768]{3,2,1,0:T(8,128)} %dynamic-slice_bitcast_fusion.5), channel_id=1, source_target_pairs={{0,4},{4,0},{8,12},{12,8},{16,20},{20,16},{24,28},{28,24},{1,5},{5... | collective-permute-start | bytes 3538952 | tf_op jit(solution)/shard_map/ppermute | solution.py:718
  486.0 20.3 %collective-permute-start.11 = (f32[96,768]{0,1:T(8,128)}, f32[96,768]{0,1:T(8,128)}, u32[]{:S(2)}, u32[]{:S(2)}) collective-permute-start(f32[96,768]{0,1:T(8,128)} %bitcast.189), channel_id=1, source_target_pairs={{0,16},{4,20},{8,24},{12,28},{16,0},{20,4},{24,8},{28,12},{1,17},{... | collective-permute-start | bytes 884744 | tf_op jit(solution)/shard_map/ppermute | solution.py:718
  489.9 19.3 %copy-start.9 = (f32[2,2,2,96,768]{4,3,2,1,0:T(8,128)S(1)}, f32[2,2,2,96,768]{4,3,2,1,0:T(8,128)}, u32[]{:S(2)}) copy-start(f32[2,2,2,96,768]{4,3,2,1,0:T(8,128)} %copy-done.8) | copy-start | bytes 7077892
  489.9 31.9 %collective-permute-start.5 = (f32[2,2,96,768]{3,2,1,0:T(8,128)S(1)}, f32[2,2,96,768]{3,2,1,0:T(8,128)S(1)}, u32[]{:S(2)}, u32[]{:S(2)}) collective-permute-start(f32[2,2,96,768]{3,2,1,0:T(8,128)S(1)} %slice_bitcast_fusion.6), channel_id=1, source_target_pairs={{0,2},{1,3},{2,0},{3,1},{4,6},{5,7},{6,4},{7,5},{8,10},{9,11},{10,... | collective-permute-start | bytes 3538952 | tf_op jit(solution)/shard_map/ppermute | solution.py:712
  498.2 20.6 %collective-permute-start.22 = (f32[2,96,768]{2,1,0:T(8,128)S(1)}, f32[2,96,768]{2,1,0:T(8,128)S(1)}, u32[]{:S(2)}, u32[]{:S(2)}) collective-permute-start(f32[2,96,768]{2,1,0:T(8,128)S(1)} %dynamic-slice_bitcast_fusion.7), channel_id=1, source_target_pairs={{0,8},{4,12},{8,0},{12,4},{16,24},{20,28},{24,16},{28,20},{1,9},{5... | collective-permute-start | bytes 1769480 | tf_op jit(solution)/shard_map/ppermute | solution.py:718
  510.7 27.0 %collective-permute-start.14 = (f32[2,96,768]{2,1,0:T(8,128)S(1)}, f32[2,96,768]{2,1,0:T(8,128)S(1)}, u32[]{:S(2)}, u32[]{:S(2)}) collective-permute-start(f32[2,96,768]{2,1,0:T(8,128)S(1)} %dynamic-slice_bitcast_fusion.9), channel_id=1, source_target_pairs={{0,8},{4,12},{8,0},{12,4},{16,24},{20,28},{24,16},{28,20},{1,9},{5... | collective-permute-start | bytes 1769480 | tf_op jit(solution)/shard_map/ppermute | solution.py:718
  518.8 19.7 %collective-permute-start.23 = (f32[96,768]{1,0:T(8,128)S(1)}, f32[96,768]{1,0:T(8,128)S(1)}, u32[]{:S(2)}, u32[]{:S(2)}) collective-permute-start(f32[96,768]{1,0:T(8,128)S(1)} %dynamic-slice_bitcast_fusion.13), channel_id=1, source_target_pairs={{0,16},{4,20},{8,24},{12,28},{16,0},{20,4},{24,8},{28,12},{1,17},{... | collective-permute-start | bytes 884744 | tf_op jit(solution)/shard_map/ppermute | solution.py:718
  522.1 16.4 %collective-permute-start.6 = (f32[2,96,768]{2,1,0:T(8,128)S(1)}, f32[2,96,768]{2,1,0:T(8,128)S(1)}, u32[]{:S(2)}, u32[]{:S(2)}) collective-permute-start(f32[2,96,768]{2,1,0:T(8,128)S(1)} %dynamic-slice_bitcast_fusion.11), channel_id=1, source_target_pairs={{0,4},{4,0},{8,12},{12,8},{16,20},{20,16},{24,28},{28,24},{1,5},{5... | collective-permute-start | bytes 1769480 | tf_op jit(solution)/shard_map/ppermute | solution.py:718
  538.5 23.9 %collective-permute-start.15 = (f32[96,768]{1,0:T(8,128)}, f32[96,768]{1,0:T(8,128)}, u32[]{:S(2)}, u32[]{:S(2)}) collective-permute-start(f32[96,768]{1,0:T(8,128)} %dynamic-slice_bitcast_fusion.15), channel_id=1, source_target_pairs={{0,16},{4,20},{8,24},{12,28},{16,0},{20,4},{24,8},{28,12},{1,17},{... | collective-permute-start | bytes 884744 | tf_op jit(solution)/shard_map/ppermute | solution.py:718
  538.8 31.8 %collective-permute-start.7 = (f32[96,768]{0,1:T(8,128)S(1)}, f32[96,768]{0,1:T(8,128)S(1)}, u32[]{:S(2)}, u32[]{:S(2)}) collective-permute-start(f32[96,768]{0,1:T(8,128)S(1)} %bitcast.190), channel_id=1, source_target_pairs={{0,16},{4,20},{8,24},{12,28},{16,0},{20,4},{24,8},{28,12},{1,17},{... | collective-permute-start | bytes 884744 | tf_op jit(solution)/shard_map/ppermute | solution.py:718
  (20 other events, 70.4 us)
